TPU v7x, 256 devices: a whole 4x4x8 slice. The times are simulated.
256 devices in a mesh: gx: 16 (over x, y), gy: 4 (over z_lo), gz: 4 (over z_hi, core).
Axes of the slice: x: 4, y: 4, z: 8 (z_hi: 2, z_lo: 4; z = z_hi * 4 + z_lo), core: 2. Of those that a mesh axis runs over, the one named last changes fastest.
Arguments:
- adjoint: float32 [19, 256, 32, 512], P(None, 'gx', 'gz', 'gy'), may hold values from -6 to 6
- density: float32 [256, 32, 512], P('gx', 'gz', 'gy'), may hold values from 0.8 to 1.2
- velocity: float32 [3, 256, 32, 512], P(None, 'gx', 'gz', 'gy'), may hold values from -0.4 to 0.4
- porosity: float32 [256, 32, 512], P('gx', 'gz', 'gy'), may hold values from 0.05 to 1
- node_type: int32 [256, 32, 512], P('gx', 'gz', 'gy'), may hold values from 0 to 2
- sensitivity_in: float32 [256, 32, 512], P('gx', 'gz', 'gy'), may hold values from -6 to 6
Outputs:
- adjoint_out: float32 [19, 256, 32, 512], P(None, 'gx', 'gz', 'gy')
- sensitivity: float32 [256, 32, 512], P('gx', 'gz', 'gy')
Inputs may be any that keep to these rules, and one draw needn't show every extreme that they name: `node_type`: 0 fluid, 1 inlet forcing, 2 fixed wall.
All inputs are finite; a program needn't handle non-finite values.
Results may differ from a plain program's by a relative error of at most 0.0001.
Values sent between devices are 32-bit elements; how exact they have to be, the bound alone decides.
A program may use at most 128 MiB of HBM per device.

v0:
```python
import functools

import jax
import jax.numpy as jnp
from jax import lax
from jax.experimental import pallas as pl
from jax.experimental.pallas import tpu as pltpu
from jax.sharding import PartitionSpec as P

AXES = ("gx", "gy", "gz")
PX, PZ, PY = 16, 8, 128
ROWS = PX * PZ

VELOCITIES = [
    (0, 0, 0),
    (1, 0, 0),
    (-1, 0, 0),
    (0, 1, 0),
    (0, -1, 0),
    (0, 0, 1),
    (0, 0, -1),
    (1, 1, 0),
    (-1, -1, 0),
    (1, -1, 0),
    (-1, 1, 0),
    (1, 0, 1),
    (-1, 0, -1),
    (1, 0, -1),
    (-1, 0, 1),
    (0, 1, 1),
    (0, -1, -1),
    (0, 1, -1),
    (0, -1, 1),
]
CROSS = [[[i for i, c in enumerate(VELOCITIES) if c[a] == s] for s in (1, -1)] for a in range(3)]
CROSS_X, CROSS_Y, CROSS_Z = CROSS
FACES_X = [(-1, 0, 0), (1, 0, 0)]
FACES_Y = [(0, -1, 0), (0, 1, 0)]
FACES_Z = [(0, 0, -1), (0, 0, 1)]
EDGES_XY = [(a, b, 0) for a in (-1, 1) for b in (-1, 1)]
EDGES_YZ = [(0, a, b) for a in (-1, 1) for b in (-1, 1)]
EDGES_XZ = [(a, 0, b) for a in (-1, 1) for b in (-1, 1)]
ROUTES = FACES_Z + EDGES_YZ + EDGES_XZ + FACES_Y + EDGES_XY + FACES_X


def side(sign):
    return (sign + 1) // 2


def collide(p, rho, u, g, node):
    ux, uy, uz = u
    e = [p[i] + p[i + 1] for i in range(1, 19, 2)]
    o = [p[i] - p[i + 1] for i in range(1, 19, 2)]
    sxy, sxz, syz = e[3] + e[4], e[5] + e[6], e[7] + e[8]
    dxy, dxz, dyz = e[3] - e[4], e[5] - e[6], e[7] - e[8]
    sx = 2.0 * e[0] + (sxy + sxz)
    sy = 2.0 * e[1] + (sxy + syz)
    sz = 2.0 * e[2] + (sxz + syz)
    trace = sx + sy + sz
    h36 = 12.0 * p[0] + (trace - (sxy + sxz + syz))
    third = h36 * (1.0 / 3.0)
    mxx, myy, mzz = sx - third, sy - third, sz - third
    hcx = 2.0 * o[0] + ((o[3] + o[4]) + (o[5] + o[6]))
    hcy = 2.0 * o[1] + ((o[3] - o[4]) + (o[7] + o[8]))
    hcz = 2.0 * o[2] + ((o[5] - o[6]) + (o[7] - o[8]))
    nx = mxx * ux + dxy * uy + dxz * uz
    ny = dxy * ux + myy * uy + dyz * uz
    nz = dxz * ux + dyz * uy + mzz * uz
    q = ux * nx + uy * ny + uz * nz
    first = ux * hcx + uy * hcy + uz * hcz
    g4 = 0.4 * g
    b = g4 * g
    a = g * (1.0 / 12.0) + (1.0 / 60.0)
    gain = rho * (first * (1.0 / 12.0) + g4 * q)
    inlet = node == 1
    wall = node == 2
    vx = a * hcx + b * nx + jnp.where(inlet, 1.0, 0.0)
    vy = a * hcy + b * ny
    vz = a * hcz + b * nz
    base = h36 * (1.1 / 36.0) + trace * (1.0 / 120.0) - (0.5 * b) * q
    ex, ey, ez = -0.025 * mxx, -0.025 * myy, -0.025 * mzz
    bx, by = base + ex, base + ey
    bz = base + ez
    bxy, bxz, byz = bx + ey, bx + ez, by + ez
    wxy, wxz, wyz = 0.05 * dxy, 0.05 * dxz, 0.05 * dyz
    even = [bx, by, bz, bxy - wxy, bxy + wxy, bxz - wxz, bxz + wxz, byz - wyz, byz + wyz]
    odd = [vx, vy, vz, vx + vy, vx - vy, vx + vz, vx - vz, vy + vz, vy - vz]
    new = [jnp.where(wall, p[0], base - 0.4 * p[0])]
    for k in range(9):
        up = even[k] - 0.2 * e[k]
        down = odd[k] - 0.1 * o[k]
        new.append(jnp.where(wall, p[2 * k + 2], up + down))
        new.append(jnp.where(wall, p[2 * k + 1], up - down))
    return new, jnp.where(wall, 0.0, gain)


def lattice_kernel(
    adj_hbm,
    rho_hbm,
    vel_hbm,
    por_hbm,
    node_hbm,
    sens_hbm,
    out_hbm,
    out_sens_hbm,
    field,
    rho,
    vel,
    por,
    node,
    sens,
    result,
    x_out,
    y_out,
    z_out,
    x_in,
    y_in,
    z_in,
    xy_in,
    yz_in,
    xz_in,
    load_sem,
    store_sem,
    send_sem,
    recv_sem,
):
    here = [lax.axis_index(a) for a in AXES]
    size = [lax.axis_size(a) for a in AXES]

    def device(route):
        return tuple(lax.rem(h + (d + n), n) if d else h for h, d, n in zip(here, route, size))

    barrier = pltpu.get_barrier_semaphore()
    for route in ROUTES:
        pl.semaphore_signal(
            barrier, inc=1, device_id=device(route), device_id_type=pl.DeviceIdType.MESH
        )
    own = pl.ds(PZ, ROWS)
    loads = [
        pltpu.make_async_copy(src, dst, load_sem.at[k])
        for k, (src, dst) in enumerate(
            [
                (adj_hbm, field.at[0, :, own, :]),
                (rho_hbm, rho),
                (vel_hbm, vel),
                (por_hbm, por),
                (node_hbm, node),
                (sens_hbm, sens),
            ]
        )
    ]
    for copy in loads:
        copy.start()

    lane = lax.broadcasted_iota(jnp.int32, (PZ, PY), 1)
    row = lax.broadcasted_iota(jnp.int32, (PZ, PY), 0)

    def plane(x):
        return pl.ds(pl.multiple_of(x * PZ, PZ), PZ)

    def columns(values, x, tiles):
        made = []
        for s in range(2):
            tile = tiles[s]
            for j, i in enumerate(CROSS_Y[s]):
                at = x + j * PX
                turned = pltpu.roll(values(i), at if s == 0 else at + 1, axis=1)
                tile = jnp.where(lane == at, turned, tile)
            made.append(tile)
        return tuple(made)

    def exchange(step, tiles):
        for s in range(2):
            y_out[step, s] = tiles[s]
            for j, i in enumerate(CROSS_Z[s]):
                z_out[step, s, j] = field[step, i, pl.ds(PZ + s * (PZ - 1), PX, stride=PZ), :]
            for j, i in enumerate(CROSS_X[s]):
                x_out[step, s, j] = field[step, i, pl.ds(PZ * (PX if s else 1), PZ), :]
        if step == 0:
            pl.semaphore_wait(barrier, len(ROUTES))
        copies = {}
        for k, route in enumerate(ROUTES):
            dx, dy, dz = route
            if route in FACES_X:
                src, dst = x_out.at[step, side(dx)], x_in.at[step, side(dx)]
            elif route in FACES_Z:
                src, dst = z_out.at[step, side(dz)], z_in.at[step, side(dz)]
            elif route in FACES_Y:
                src, dst = y_out.at[step, side(dy)], y_in.at[step, side(dy)]
            elif route in EDGES_XY:
                src, dst = y_out.at[step, side(dy)], xy_in.at[step, side(dx), side(dy)]
            elif route in EDGES_YZ:
                src, dst = y_out.at[step, side(dy)], yz_in.at[step, side(dy), side(dz)]
            else:
                j = CROSS_Z[side(dz)].index(VELOCITIES.index((-dx, 0, -dz)))
                src = z_out.at[step, side(dz), j, pl.ds(side(dx) * (PX - 8), 8), :]
                dst = xz_in.at[step, side(dx), side(dz)]
            copy = pltpu.make_async_remote_copy(
                src_ref=src,
                dst_ref=dst,
                send_sem=send_sem.at[step, k],
                recv_sem=recv_sem.at[step, k],
                device_id=device(route),
                device_id_type=pl.DeviceIdType.MESH,
            )
            copy.start()
            copies[route] = copy
        return copies

    def insert(step, copies):
        for route in ROUTES:
            copies[route].wait_recv()
        for s in range(2):
            for j, i in enumerate(CROSS_X[s]):
                field[step, i, pl.ds(0 if s else PZ * (PX + 1), PZ), :] = x_in[step, s, j]
            for j, i in enumerate(CROSS_Z[s]):
                field[step, i, pl.ds(PZ + s * (PZ - 1), PX, stride=PZ), :] = z_in[step, s, j]
        for dx, _, dz in EDGES_XZ:
            i = VELOCITIES.index((-dx, 0, -dz))
            at = (0 if dx == 1 else PZ * (PX + 1)) + side(dz) * (PZ - 1)
            field[step, i, pl.ds(at, 1), :] = xz_in[
                step, side(dx), side(dz), pl.ds(side(dx) * (PZ - 1), 1), :
            ]
        halos = []
        for s in range(2):
            tile = y_in[step, s]
            halo = tile
            for j, i in enumerate(CROSS_Y[s]):
                cx, _, cz = VELOCITIES[i]
                if cx:
                    corner = xy_in[step, side(-cx), s]
                    shifted = pltpu.roll(tile, PY - 1 if cx == 1 else 1, axis=1)
                    corner = pltpu.roll(corner, PX - 1 if cx == 1 else PY - PX + 1, axis=1)
                    shifted = jnp.where(
                        lane == j * PX + (PX - 1 if cx == 1 else 0), corner, shifted
                    )
                elif cz:
                    corner = yz_in[step, s, side(-cz)]
                    shifted = jnp.where(row == (0 if cz == 1 else PZ - 1), corner, tile)
                    shifted = pltpu.roll(shifted, PZ - 1 if cz == 1 else 1, axis=0)
                else:
                    continue
                halo = jnp.where(
                    jnp.logical_and(lane >= j * PX, lane < (j + 1) * PX), shifted, halo
                )
            halos.append(halo)
        return halos

    def advance(step, halos, x):
        pulled = []
        for i, (cx, cy, cz) in enumerate(VELOCITIES):
            value = field[step, i, plane(x + (1 + cx)), :]
            if cz:
                value = pltpu.roll(value, PZ - 1 if cz == 1 else 1, axis=0)
            if cy:
                s = 0 if cy == 1 else 1
                at = CROSS_Y[s].index(i) * PX + x
                edge = PY - 1 if cy == 1 else 0
                value = pltpu.roll(value, PY - 1 if cy == 1 else 1, axis=1)
                column = pltpu.roll(halos[s], lax.rem(edge + PY - at, PY), axis=1)
                value = jnp.where(lane == edge, column, value)
            pulled.append(value)
        here_rows = plane(x)
        u = [vel[d, here_rows, :] for d in range(3)]
        new, gain = collide(
            pulled, rho[here_rows, :], u, por[here_rows, :], node[here_rows, :]
        )
        sens[here_rows, :] = sens[here_rows, :] + gain
        return new

    blank = (jnp.zeros((PZ, PY), jnp.float32),) * 2
    loads[0].wait()
    tiles = lax.fori_loop(
        0,
        PX,
        lambda x, t: columns(lambda i: field[0, i, plane(x + 1), :], x, t),
        blank,
    )
    first = exchange(0, tiles)
    for copy in loads[1:]:
        copy.wait()
    halos = insert(0, first)

    def first_step(x, t):
        new = advance(0, halos, x)
        for i in range(19):
            field[1, i, plane(x + 1), :] = new[i]
        return columns(lambda i: new[i], x, t)

    tiles = lax.fori_loop(0, PX, first_step, blank)
    second = exchange(1, tiles)
    halos = insert(1, second)

    stores = []
    parts = 4
    for part in range(parts):

        def second_step(x, _):
            new = advance(1, halos, x)
            for i in range(19):
                result[i, plane(x), :] = new[i]
            return _

        lax.fori_loop(part * PX // parts, (part + 1) * PX // parts, second_step, 0)
        span = pl.ds(part * ROWS // parts, ROWS // parts)
        stores.append(
            pltpu.make_async_copy(
                result.at[:, span, :], out_hbm.at[:, span, :], store_sem.at[part]
            )
        )
        stores[-1].start()
    stores.append(pltpu.make_async_copy(sens, out_sens_hbm, store_sem.at[parts]))
    stores[-1].start()
    for copies in (first, second):
        for route in ROUTES:
            copies[route].wait_send()
    for copy in stores:
        copy.wait()


def shards(adjoint, density, velocity, porosity, node_type, sensitivity_in):
    f32 = jnp.float32
    dma = pltpu.SemaphoreType.DMA
    anywhere = pl.BlockSpec(memory_space=pl.ANY)
    out, sens = pl.pallas_call(
        lattice_kernel,
        out_shape=(
            jax.ShapeDtypeStruct((19, ROWS, PY), f32),
            jax.ShapeDtypeStruct((ROWS, PY), f32),
        ),
        in_specs=[anywhere] * 6,
        out_specs=(anywhere, anywhere),
        scratch_shapes=[
            pltpu.VMEM((2, 19, ROWS + 2 * PZ, PY), f32),
            pltpu.VMEM((ROWS, PY), f32),
            pltpu.VMEM((3, ROWS, PY), f32),
            pltpu.VMEM((ROWS, PY), f32),
            pltpu.VMEM((ROWS, PY), jnp.int32),
            pltpu.VMEM((ROWS, PY), f32),
            pltpu.VMEM((19, ROWS, PY), f32),
            pltpu.VMEM((2, 2, 5, PZ, PY), f32),
            pltpu.VMEM((2, 2, PZ, PY), f32),
            pltpu.VMEM((2, 2, 5, PX, PY), f32),
            pltpu.VMEM((2, 2, 5, PZ, PY), f32),
            pltpu.VMEM((2, 2, PZ, PY), f32),
            pltpu.VMEM((2, 2, 5, PX, PY), f32),
            pltpu.VMEM((2, 2, 2, PZ, PY), f32),
            pltpu.VMEM((2, 2, 2, PZ, PY), f32),
            pltpu.VMEM((2, 2, 2, PZ, PY), f32),
            dma((6,)),
            dma((5,)),
            dma((2, len(ROUTES))),
            dma((2, len(ROUTES))),
        ],
        compiler_params=pltpu.CompilerParams(
            collective_id=0, has_side_effects=True, vmem_limit_bytes=32 * 1024 * 1024
        ),
    )(
        adjoint.reshape(19, ROWS, PY),
        density.reshape(ROWS, PY),
        velocity.reshape(3, ROWS, PY),
        porosity.reshape(ROWS, PY),
        node_type.reshape(ROWS, PY),
        sensitivity_in.reshape(ROWS, PY),
    )
    return out.reshape(19, PX, PZ, PY), sens.reshape(PX, PZ, PY)


def solution(mesh):
    cells = P("gx", "gz", "gy")
    many = P(None, "gx", "gz", "gy")
    return jax.shard_map(
        shards,
        mesh=mesh,
        in_specs=(many, cells, many, cells, cells, cells),
        out_specs=(many, cells),
        check_vma=False,
    )
```

profile of v0, /device:TPU:1, one launch (start us, length us, event | category | flops | bytes accessed | tf_op | source)
XLA Modules:
  0.0 43.2 jit_solution(17568458562226946212)
XLA Ops:
  0.6 0.0 copy-start
  0.6 1.3 %copy-done = f32[19,16,8,128]{3,2,1,0:T(8,128)S(1)} copy-done((f32[19,16,8,128]{3,2,1,0:T(8,128)S(1)}, f32[19,16,8,128]{3,2,1,0:T(8,128)}, u32[]{:S(2)}) %copy-start) | copy-done | bytes 1245208
  1.9 0.0 copy-start.1
  1.9 0.9 %copy-done.1 = f32[3,16,8,128]{3,2,1,0:T(8,128)S(1)} copy-done((f32[3,16,8,128]{3,2,1,0:T(8,128)S(1)}, f32[3,16,8,128]{3,2,1,0:T(8,128)}, u32[]{:S(2)}) %copy-start.1) | copy-done | bytes 196632
  2.9 0.0 copy-start.2
  2.9 0.8 %copy-done.2 = f32[16,8,128]{2,1,0:T(8,128)S(1)} copy-done((f32[16,8,128]{2,1,0:T(8,128)S(1)}, f32[16,8,128]{2,1,0:T(8,128)}, u32[]{:S(2)}) %copy-start.2) | copy-done | bytes 65560
  3.7 0.0 copy-start.3
  3.7 0.8 %copy-done.3 = f32[16,8,128]{2,1,0:T(8,128)S(1)} copy-done((f32[16,8,128]{2,1,0:T(8,128)S(1)}, f32[16,8,128]{2,1,0:T(8,128)}, u32[]{:S(2)}) %copy-start.3) | copy-done | bytes 65560
  4.5 0.0 copy-start.4
  4.5 0.8 %copy-done.4 = s32[16,8,128]{2,1,0:T(8,128)S(1)} copy-done((s32[16,8,128]{2,1,0:T(8,128)S(1)}, s32[16,8,128]{2,1,0:T(8,128)}, u32[]{:S(2)}) %copy-start.4) | copy-done | bytes 65560
  5.4 0.0 copy-start.5
  5.4 0.8 %copy-done.5 = f32[16,8,128]{2,1,0:T(8,128)S(1)} copy-done((f32[16,8,128]{2,1,0:T(8,128)S(1)}, f32[16,8,128]{2,1,0:T(8,128)}, u32[]{:S(2)}) %copy-start.5) | copy-done | bytes 65560
  6.2 35.4 %shard_map.77 = (f32[19,128,128]{2,1,0:T(8,128)S(1)}, f32[128,128]{1,0:T(8,128)S(1)}) custom-call(f32[19,128,128]{2,1,0:T(8,128)S(1)} %bitcast.9, f32[128,128]{1,0:T(8,128)S(1)} %bitcast.12, f32[3,128,128]{2,1,0:T(8,128)S(1)} %bitcast.10, f32[128,128]{1,0:T(8,128)S(1)} %bitcast.13, s32[128,128]{1,0:T(8,128)S(1)} %bitcast.14, f32[128,128]{1,0:T(8,128)S(1)} %bitcast.15), custom_call_target="tpu_custom_call" | custom-call | tf_op jit(solution)/shard_map/pallas_call | solution.py:325
  41.6 1.0 %copy.10 = f32[19,16,8,128]{3,2,1,0:T(8,128)} copy(f32[19,16,8,128]{3,2,1,0:T(8,128)S(1)} %bitcast.8) | data formatting | bytes 2490368
  42.6 0.6 %copy.11 = f32[16,8,128]{2,1,0:T(8,128)} copy(f32[16,8,128]{2,1,0:T(8,128)S(1)} %bitcast.11) | data formatting | bytes 131072
Async XLA Ops:
  0.6 1.3 %copy-start = (f32[19,16,8,128]{3,2,1,0:T(8,128)S(1)}, f32[19,16,8,128]{3,2,1,0:T(8,128)}, u32[]{:S(2)}) copy-start(f32[19,16,8,128]{3,2,1,0:T(8,128)} %param.6) | copy-start | bytes 3735556
  1.9 0.9 %copy-start.1 = (f32[3,16,8,128]{3,2,1,0:T(8,128)S(1)}, f32[3,16,8,128]{3,2,1,0:T(8,128)}, u32[]{:S(2)}) copy-start(f32[3,16,8,128]{3,2,1,0:T(8,128)} %param.8) | copy-start | bytes 589828
  2.9 0.8 %copy-start.2 = (f32[16,8,128]{2,1,0:T(8,128)S(1)}, f32[16,8,128]{2,1,0:T(8,128)}, u32[]{:S(2)}) copy-start(f32[16,8,128]{2,1,0:T(8,128)} %param.7) | copy-start | bytes 196612
  3.7 0.8 %copy-start.3 = (f32[16,8,128]{2,1,0:T(8,128)S(1)}, f32[16,8,128]{2,1,0:T(8,128)}, u32[]{:S(2)}) copy-start(f32[16,8,128]{2,1,0:T(8,128)} %param.9) | copy-start | bytes 196612
  4.5 0.8 %copy-start.4 = (s32[16,8,128]{2,1,0:T(8,128)S(1)}, s32[16,8,128]{2,1,0:T(8,128)}, u32[]{:S(2)}) copy-start(s32[16,8,128]{2,1,0:T(8,128)} %param.10) | copy-start | bytes 196612
  5.4 0.8 %copy-start.5 = (f32[16,8,128]{2,1,0:T(8,128)S(1)}, f32[16,8,128]{2,1,0:T(8,128)}, u32[]{:S(2)}) copy-start(f32[16,8,128]{2,1,0:T(8,128)} %param.11) | copy-start | bytes 196612
where the time goes:
time: 43.6 us; the launch traced here: 43.2 us
  Pallas kernels  35.4 us (81%)
  local copies, waits for them, and re-layouts  7.23 us (17%)
  between operations  0.65 us (1%)
    pallas_call x1, Pallas kernels, shards(): pl.pallas_call(lattice_kernel, out_shape=(jax.ShapeDtypeStruct((19, ROWS,...  35.4 us
    unnamed x14, local copies, waits for them, and re-layouts  7.23 us

commit v1 on v0

--- a/solution.py
+++ b/solution.py
@@ -40,7 +40,7 @@
 EDGES_XY = [(a, b, 0) for a in (-1, 1) for b in (-1, 1)]
 EDGES_YZ = [(0, a, b) for a in (-1, 1) for b in (-1, 1)]
 EDGES_XZ = [(a, 0, b) for a in (-1, 1) for b in (-1, 1)]
-ROUTES = FACES_Z + EDGES_YZ + EDGES_XZ + FACES_Y + EDGES_XY + FACES_X
+ROUTES = EDGES_XZ + EDGES_XY + EDGES_YZ + FACES_Y + FACES_X + FACES_Z
 
 
 def side(sign):
@@ -101,15 +101,13 @@
     por_hbm,
     node_hbm,
     sens_hbm,
-    out_hbm,
-    out_sens_hbm,
+    result,
+    sens,
     field,
     rho,
     vel,
     por,
     node,
-    sens,
-    result,
     x_out,
     y_out,
     z_out,
@@ -120,7 +118,6 @@
     yz_in,
     xz_in,
     load_sem,
-    store_sem,
     send_sem,
     recv_sem,
 ):
@@ -275,6 +272,7 @@
         PX,
         lambda x, t: columns(lambda i: field[0, i, plane(x + 1), :], x, t),
         blank,
+        unroll=4,
     )
     first = exchange(0, tiles)
     for copy in loads[1:]:
@@ -287,35 +285,20 @@
             field[1, i, plane(x + 1), :] = new[i]
         return columns(lambda i: new[i], x, t)
 
-    tiles = lax.fori_loop(0, PX, first_step, blank)
+    tiles = lax.fori_loop(0, PX, first_step, blank, unroll=4)
     second = exchange(1, tiles)
     halos = insert(1, second)
 
-    stores = []
-    parts = 4
-    for part in range(parts):
-
-        def second_step(x, _):
-            new = advance(1, halos, x)
-            for i in range(19):
-                result[i, plane(x), :] = new[i]
-            return _
-
-        lax.fori_loop(part * PX // parts, (part + 1) * PX // parts, second_step, 0)
-        span = pl.ds(part * ROWS // parts, ROWS // parts)
-        stores.append(
-            pltpu.make_async_copy(
-                result.at[:, span, :], out_hbm.at[:, span, :], store_sem.at[part]
-            )
-        )
-        stores[-1].start()
-    stores.append(pltpu.make_async_copy(sens, out_sens_hbm, store_sem.at[parts]))
-    stores[-1].start()
+    def second_step(x, carry):
+        new = advance(1, halos, x)
+        for i in range(19):
+            result[i, plane(x), :] = new[i]
+        return carry
+
+    lax.fori_loop(0, PX, second_step, 0, unroll=4)
     for copies in (first, second):
         for route in ROUTES:
             copies[route].wait_send()
-    for copy in stores:
-        copy.wait()
 
 
 def shards(adjoint, density, velocity, porosity, node_type, sensitivity_in):
@@ -325,19 +308,17 @@
     out, sens = pl.pallas_call(
         lattice_kernel,
         out_shape=(
-            jax.ShapeDtypeStruct((19, ROWS, PY), f32),
-            jax.ShapeDtypeStruct((ROWS, PY), f32),
+            pltpu.VMEM((19, ROWS, PY), f32),
+            pltpu.VMEM((ROWS, PY), f32),
         ),
         in_specs=[anywhere] * 6,
-        out_specs=(anywhere, anywhere),
+        out_specs=(pl.BlockSpec(memory_space=pltpu.VMEM),) * 2,
         scratch_shapes=[
             pltpu.VMEM((2, 19, ROWS + 2 * PZ, PY), f32),
             pltpu.VMEM((ROWS, PY), f32),
             pltpu.VMEM((3, ROWS, PY), f32),
             pltpu.VMEM((ROWS, PY), f32),
             pltpu.VMEM((ROWS, PY), jnp.int32),
-            pltpu.VMEM((ROWS, PY), f32),
-            pltpu.VMEM((19, ROWS, PY), f32),
             pltpu.VMEM((2, 2, 5, PZ, PY), f32),
             pltpu.VMEM((2, 2, PZ, PY), f32),
             pltpu.VMEM((2, 2, 5, PX, PY), f32),
@@ -348,12 +329,11 @@
             pltpu.VMEM((2, 2, 2, PZ, PY), f32),
             pltpu.VMEM((2, 2, 2, PZ, PY), f32),
             dma((6,)),
-            dma((5,)),
             dma((2, len(ROUTES))),
             dma((2, len(ROUTES))),
         ],
         compiler_params=pltpu.CompilerParams(
-            collective_id=0, has_side_effects=True, vmem_limit_bytes=32 * 1024 * 1024
+            collective_id=0, has_side_effects=True, vmem_limit_bytes=56 * 1024 * 1024
         ),
     )(
         adjoint.reshape(19, ROWS, PY),

time: 43.6 us -> 32.1 us (0.74)
  Pallas kernels: 35.4 us -> 29.7 us
  local copies, waits for them, and re-layouts: 7.23 us -> 1.67 us
    pallas_call x1, Pallas kernels: 35.4 us -> 29.7 us  [shards(): pl.pallas_call(lattice_kernel, out_shape=(pltpu.VMEM((19, ROWS, PY), f32)...]
    unnamed x14 -> x2, local copies, waits for them, and re-layouts: 7.23 us -> 1.67 us
where the time goes in v1:
time: 32.1 us; the launch traced here: 32 us
  Pallas kernels  29.7 us (93%)
  local copies, waits for them, and re-layouts  1.67 us (5%)
  between operations  0.64 us (2%)
    pallas_call x1, Pallas kernels, shards(): pl.pallas_call(lattice_kernel, out_shape=(pltpu.VMEM((19, ROWS, PY), f32)...  29.7 us
    unnamed x2, local copies, waits for them, and re-layouts  1.67 us

profile of v1, /device:TPU:1, one launch (start us, length us, event | category | flops | bytes accessed | tf_op | source)
XLA Modules:
  0.0 32.0 jit_solution(11366063300473974729)
XLA Ops:
  0.6 29.7 %shard_map.77 = (f32[19,128,128]{2,1,0:T(8,128)S(1)}, f32[128,128]{1,0:T(8,128)S(1)}) custom-call(f32[19,128,128]{2,1,0:T(8,128)} %bitcast.10, f32[128,128]{1,0:T(8,128)} %bitcast.12, f32[3,128,128]{2,1,0:T(8,128)} %bitcast.11, f32[128,128]{1,0:T(8,128)} %bitcast.13, s32[128,128]{1,0:T(8,128)} %bitcast.14, f32[128,128]{1,0:T(8,128)} %bitcast.15), custom_call_target="tpu_custom_call" | custom-call | tf_op jit(solution)/shard_map/pallas_call | solution.py:308
  30.3 1.0 %copy.10 = f32[19,16,8,128]{3,2,1,0:T(8,128)} copy(f32[19,16,8,128]{3,2,1,0:T(8,128)S(1)} %bitcast.8) | data formatting | bytes 2490368
  31.3 0.6 %copy.11 = f32[16,8,128]{2,1,0:T(8,128)} copy(f32[16,8,128]{2,1,0:T(8,128)S(1)} %bitcast.9) | data formatting | bytes 131072

commit v2 on v1

--- a/solution.py
+++ b/solution.py
@@ -40,7 +40,7 @@
 EDGES_XY = [(a, b, 0) for a in (-1, 1) for b in (-1, 1)]
 EDGES_YZ = [(0, a, b) for a in (-1, 1) for b in (-1, 1)]
 EDGES_XZ = [(a, 0, b) for a in (-1, 1) for b in (-1, 1)]
-ROUTES = EDGES_XZ + EDGES_XY + EDGES_YZ + FACES_Y + FACES_X + FACES_Z
+ROUTES = EDGES_XZ + EDGES_XY + FACES_Z + EDGES_YZ + FACES_Y + FACES_X
 
 
 def side(sign):
@@ -153,18 +153,29 @@
     row = lax.broadcasted_iota(jnp.int32, (PZ, PY), 0)
 
     def plane(x):
+        if isinstance(x, int):
+            return pl.ds(x * PZ, PZ)
         return pl.ds(pl.multiple_of(x * PZ, PZ), PZ)
 
-    def columns(values, x, tiles):
+    def pack_columns(step, x, tiles):
         made = []
         for s in range(2):
             tile = tiles[s]
             for j, i in enumerate(CROSS_Y[s]):
                 at = x + j * PX
-                turned = pltpu.roll(values(i), at if s == 0 else at + 1, axis=1)
+                value = field[step, i, plane(x + 1), :]
+                turned = pltpu.roll(value, at if s == 0 else at + 1, axis=1)
                 tile = jnp.where(lane == at, turned, tile)
             made.append(tile)
         return tuple(made)
+
+    def put_column(step, i, x, tile, at):
+        edge = 0 if VELOCITIES[i][1] == 1 else PY - 1
+        shift = (edge - at) % PY if isinstance(at, int) else edge + PY - at
+        column = pltpu.roll(tile, shift, axis=1)
+        field[step, i, plane(x + 1), :] = jnp.where(
+            lane == edge, column, field[step, i, plane(x + 1), :]
+        )
 
     def exchange(step, tiles):
         for s in range(2):
@@ -204,58 +215,67 @@
             copies[route] = copy
         return copies
 
-    def insert(step, copies):
-        for route in ROUTES:
+    def insert_y(step, copies):
+        for route in FACES_Y + EDGES_YZ:
+            copies[route].wait_recv()
+        tiles = {}
+        for s in range(2):
+            for i in CROSS_Y[s]:
+                cz = VELOCITIES[i][2]
+                tiles[i] = y_in[step, s]
+                if cz:
+                    tiles[i] = jnp.where(
+                        row == (0 if cz == 1 else PZ - 1), yz_in[step, s, side(-cz)], tiles[i]
+                    )
+
+        def body(x, carry):
+            for s in range(2):
+                for j, i in enumerate(CROSS_Y[s]):
+                    put_column(step, i, x, tiles[i], x + j * PX)
+            return carry
+
+        lax.fori_loop(0, PX, body, 0, unroll=4)
+
+    def insert_z(step, copies):
+        for route in FACES_Z:
+            copies[route].wait_recv()
+        wide = lax.broadcasted_iota(jnp.int32, (PX, PY), 1)
+        for s in range(2):
+            for j, i in enumerate(CROSS_Z[s]):
+                rows = pl.ds(PZ + s * (PZ - 1), PX, stride=PZ)
+                value = z_in[step, s, j]
+                cy = VELOCITIES[i][1]
+                if cy:
+                    value = jnp.where(
+                        wide == (0 if cy == 1 else PY - 1), field[step, i, rows, :], value
+                    )
+                field[step, i, rows, :] = value
+
+    def insert_x(step, copies):
+        for route in FACES_X + EDGES_XY + EDGES_XZ:
             copies[route].wait_recv()
         for s in range(2):
             for j, i in enumerate(CROSS_X[s]):
-                field[step, i, pl.ds(0 if s else PZ * (PX + 1), PZ), :] = x_in[step, s, j]
-            for j, i in enumerate(CROSS_Z[s]):
-                field[step, i, pl.ds(PZ + s * (PZ - 1), PX, stride=PZ), :] = z_in[step, s, j]
+                field[step, i, plane(0 if s else PX + 1), :] = x_in[step, s, j]
         for dx, _, dz in EDGES_XZ:
             i = VELOCITIES.index((-dx, 0, -dz))
             at = (0 if dx == 1 else PZ * (PX + 1)) + side(dz) * (PZ - 1)
             field[step, i, pl.ds(at, 1), :] = xz_in[
                 step, side(dx), side(dz), pl.ds(side(dx) * (PZ - 1), 1), :
             ]
-        halos = []
-        for s in range(2):
-            tile = y_in[step, s]
-            halo = tile
-            for j, i in enumerate(CROSS_Y[s]):
-                cx, _, cz = VELOCITIES[i]
-                if cx:
-                    corner = xy_in[step, side(-cx), s]
-                    shifted = pltpu.roll(tile, PY - 1 if cx == 1 else 1, axis=1)
-                    corner = pltpu.roll(corner, PX - 1 if cx == 1 else PY - PX + 1, axis=1)
-                    shifted = jnp.where(
-                        lane == j * PX + (PX - 1 if cx == 1 else 0), corner, shifted
-                    )
-                elif cz:
-                    corner = yz_in[step, s, side(-cz)]
-                    shifted = jnp.where(row == (0 if cz == 1 else PZ - 1), corner, tile)
-                    shifted = pltpu.roll(shifted, PZ - 1 if cz == 1 else 1, axis=0)
-                else:
-                    continue
-                halo = jnp.where(
-                    jnp.logical_and(lane >= j * PX, lane < (j + 1) * PX), shifted, halo
-                )
-            halos.append(halo)
-        return halos
-
-    def advance(step, halos, x):
+        for dx, dy, _ in EDGES_XY:
+            i = VELOCITIES.index((-dx, -dy, 0))
+            at = CROSS_Y[side(dy)].index(i) * PX + (PX - 1 if dx == 1 else 0)
+            put_column(step, i, -1 if dx == 1 else PX, xy_in[step, side(dx), side(dy)], at)
+
+    def advance(step, x):
         pulled = []
         for i, (cx, cy, cz) in enumerate(VELOCITIES):
             value = field[step, i, plane(x + (1 + cx)), :]
             if cz:
                 value = pltpu.roll(value, PZ - 1 if cz == 1 else 1, axis=0)
             if cy:
-                s = 0 if cy == 1 else 1
-                at = CROSS_Y[s].index(i) * PX + x
-                edge = PY - 1 if cy == 1 else 0
                 value = pltpu.roll(value, PY - 1 if cy == 1 else 1, axis=1)
-                column = pltpu.roll(halos[s], lax.rem(edge + PY - at, PY), axis=1)
-                value = jnp.where(lane == edge, column, value)
             pulled.append(value)
         here_rows = plane(x)
         u = [vel[d, here_rows, :] for d in range(3)]
@@ -265,47 +285,65 @@
         sens[here_rows, :] = sens[here_rows, :] + gain
         return new
 
+    def first_step(x, carry):
+        new = advance(0, x)
+        for i in range(19):
+            field[1, i, plane(x + 1), :] = new[i]
+        return carry
+
+    def second_step(x, carry):
+        new = advance(1, x)
+        for i in range(19):
+            result[i, plane(x), :] = new[i]
+        return carry
+
+    def pack(step, low, high, tiles):
+        return lax.fori_loop(
+            low, high, lambda x, t: pack_columns(step, x, t), tiles, unroll=high - low
+        )
+
     blank = (jnp.zeros((PZ, PY), jnp.float32),) * 2
     loads[0].wait()
-    tiles = lax.fori_loop(
-        0,
-        PX,
-        lambda x, t: columns(lambda i: field[0, i, plane(x + 1), :], x, t),
-        blank,
-        unroll=4,
-    )
+    tiles = pack(0, 0, PX, blank)
     first = exchange(0, tiles)
     for copy in loads[1:]:
         copy.wait()
-    halos = insert(0, first)
-
-    def first_step(x, t):
-        new = advance(0, halos, x)
-        for i in range(19):
-            field[1, i, plane(x + 1), :] = new[i]
-        return columns(lambda i: new[i], x, t)
-
-    tiles = lax.fori_loop(0, PX, first_step, blank, unroll=4)
+    insert_y(0, first)
+    insert_z(0, first)
+    lax.fori_loop(1, PX - 1, first_step, 0, unroll=7)
+    tiles = pack(1, 1, PX - 1, blank)
+    insert_x(0, first)
+    for x in (0, PX - 1):
+        first_step(x, 0)
+        tiles = pack_columns(1, x, tiles)
     second = exchange(1, tiles)
-    halos = insert(1, second)
-
-    def second_step(x, carry):
-        new = advance(1, halos, x)
-        for i in range(19):
-            result[i, plane(x), :] = new[i]
-        return carry
-
-    lax.fori_loop(0, PX, second_step, 0, unroll=4)
+    insert_y(1, second)
+    insert_z(1, second)
+    lax.fori_loop(1, PX - 1, second_step, 0, unroll=7)
+    insert_x(1, second)
+    for x in (0, PX - 1):
+        second_step(x, 0)
     for copies in (first, second):
         for route in ROUTES:
             copies[route].wait_send()
+
+
+def store_kernel(result, sens, out_hbm, out_sens_hbm, sem):
+    copies = [
+        pltpu.make_async_copy(result, out_hbm, sem.at[0]),
+        pltpu.make_async_copy(sens, out_sens_hbm, sem.at[1]),
+    ]
+    for copy in copies:
+        copy.start()
+    for copy in copies:
+        copy.wait()
 
 
 def shards(adjoint, density, velocity, porosity, node_type, sensitivity_in):
     f32 = jnp.float32
     dma = pltpu.SemaphoreType.DMA
     anywhere = pl.BlockSpec(memory_space=pl.ANY)
-    out, sens = pl.pallas_call(
+    made = pl.pallas_call(
         lattice_kernel,
         out_shape=(
             pltpu.VMEM((19, ROWS, PY), f32),
@@ -343,6 +381,17 @@
         node_type.reshape(ROWS, PY),
         sensitivity_in.reshape(ROWS, PY),
     )
+    out, sens = pl.pallas_call(
+        store_kernel,
+        out_shape=(
+            jax.ShapeDtypeStruct((19, ROWS, PY), f32),
+            jax.ShapeDtypeStruct((ROWS, PY), f32),
+        ),
+        in_specs=[anywhere] * 2,
+        out_specs=(anywhere, anywhere),
+        scratch_shapes=[dma((2,))],
+        compiler_params=pltpu.CompilerParams(vmem_limit_bytes=1024 * 1024),
+    )(*made)
     return out.reshape(19, PX, PZ, PY), sens.reshape(PX, PZ, PY)
 
 

time: 32.1 us -> 30 us (0.935)
  local copies, waits for them, and re-layouts: 1.67 us -> 0 us
  Pallas kernels: 29.7 us -> 29.3 us
    unnamed x2 -> x0, local copies, waits for them, and re-layouts: 1.67 us -> none
    pallas_call x1, Pallas kernels: 29.7 us -> 28.2 us  [shards(): pl.pallas_call(lattice_kernel, out_shape=(pltpu.VMEM((19, ROWS, PY), f32)...]
    pallas_call x0 -> x1, Pallas kernels: none -> 1.06 us  [shards(): pl.pallas_call(store_kernel, out_shape=(jax.ShapeDtypeStruct((19, ROWS, P...]
where the time goes in v2:
time: 30 us; the launch traced here: 29.9 us
  Pallas kernels  29.3 us (98%)
  between operations  0.64 us (2%)
    pallas_call x1, Pallas kernels, shards(): pl.pallas_call(lattice_kernel, out_shape=(pltpu.VMEM((19, ROWS, PY), f32)...  28.2 us
    pallas_call x1, Pallas kernels, shards(): pl.pallas_call(store_kernel, out_shape=(jax.ShapeDtypeStruct((19, ROWS, P...  1.06 us

profile of v2, /device:TPU:1, one launch (start us, length us, event | category | flops | bytes accessed | tf_op | source)
XLA Modules:
  0.0 29.9 jit_solution(950609072738862775)
XLA Ops:
  0.6 28.2 %shard_map.77 = (f32[19,128,128]{2,1,0:T(8,128)S(1)}, f32[128,128]{1,0:T(8,128)S(1)}) custom-call(f32[19,128,128]{2,1,0:T(8,128)} %bitcast.8, f32[128,128]{1,0:T(8,128)} %bitcast.10, f32[3,128,128]{2,1,0:T(8,128)} %bitcast.9, f32[128,128]{1,0:T(8,128)} %bitcast.11, s32[128,128]{1,0:T(8,128)} %bitcast.12, f32[128,128]{1,0:T(8,128)} %bitcast.13), custom_call_target="tpu_custom_call" | custom-call | tf_op jit(solution)/shard_map/pallas_call | solution.py:346
  28.9 1.1 %shard_map.78 = (f32[19,128,128]{2,1,0:T(8,128)}, f32[128,128]{1,0:T(8,128)}) custom-call(f32[19,128,128]{2,1,0:T(8,128)S(1)} %get-tuple-element.6.result, f32[128,128]{1,0:T(8,128)S(1)} %get-tuple-element.7.sens), custom_call_target="tpu_custom_call" | custom-call | tf_op jit(solution)/shard_map/pallas_call | solution.py:384

commit v3 on v2

--- a/solution.py
+++ b/solution.py
@@ -40,7 +40,9 @@
 EDGES_XY = [(a, b, 0) for a in (-1, 1) for b in (-1, 1)]
 EDGES_YZ = [(0, a, b) for a in (-1, 1) for b in (-1, 1)]
 EDGES_XZ = [(a, 0, b) for a in (-1, 1) for b in (-1, 1)]
-ROUTES = EDGES_XZ + EDGES_XY + FACES_Z + EDGES_YZ + FACES_Y + FACES_X
+FAR = EDGES_XZ + EDGES_XY + FACES_X
+NEAR = FACES_Z + EDGES_YZ + FACES_Y
+ROUTES = FAR + NEAR
 
 
 def side(sign):
@@ -101,9 +103,8 @@
     por_hbm,
     node_hbm,
     sens_hbm,
-    result,
+    field,
     sens,
-    field,
     rho,
     vel,
     por,
@@ -111,6 +112,8 @@
     x_out,
     y_out,
     z_out,
+    xy_out,
+    xz_out,
     x_in,
     y_in,
     z_in,
@@ -142,7 +145,7 @@
                 (vel_hbm, vel),
                 (por_hbm, por),
                 (node_hbm, node),
-                (sens_hbm, sens),
+                (sens_hbm, sens.at[0]),
             ]
         )
     ]
@@ -169,55 +172,62 @@
             made.append(tile)
         return tuple(made)
 
-    def put_column(step, i, x, tile, at):
-        edge = 0 if VELOCITIES[i][1] == 1 else PY - 1
-        shift = (edge - at) % PY if isinstance(at, int) else edge + PY - at
+    def pull_y(step, i, x, tile, at):
+        cy = VELOCITIES[i][1]
+        edge = PY - 1 if cy == 1 else 0
+        shift = (edge - at) % PY if isinstance(at, int) else (edge or PY) - at
         column = pltpu.roll(tile, shift, axis=1)
-        field[step, i, plane(x + 1), :] = jnp.where(
-            lane == edge, column, field[step, i, plane(x + 1), :]
+        value = pltpu.roll(field[step, i, plane(x + 1), :], PY - 1 if cy == 1 else 1, axis=1)
+        field[step, i, plane(x + 1), :] = jnp.where(lane == edge, column, value)
+
+    def transfer(step, route):
+        dx, dy, dz = route
+        if route in FACES_X:
+            src, dst = x_out.at[step, side(dx)], x_in.at[step, side(dx)]
+        elif route in FACES_Z:
+            src, dst = z_out.at[step, side(dz)], z_in.at[step, side(dz)]
+        elif route in FACES_Y:
+            src, dst = y_out.at[step, side(dy)], y_in.at[step, side(dy)]
+        elif route in EDGES_XY:
+            src, dst = xy_out.at[step, side(dy)], xy_in.at[step, side(dx), side(dy)]
+        elif route in EDGES_YZ:
+            src, dst = y_out.at[step, side(dy)], yz_in.at[step, side(dy), side(dz)]
+        else:
+            src, dst = xz_out.at[step, side(dx)], xz_in.at[step, side(dx), side(dz)]
+        k = ROUTES.index(route)
+        return pltpu.make_async_remote_copy(
+            src_ref=src,
+            dst_ref=dst,
+            send_sem=send_sem.at[step, k],
+            recv_sem=recv_sem.at[step, k],
+            device_id=device(route),
+            device_id_type=pl.DeviceIdType.MESH,
         )
 
-    def exchange(step, tiles):
+    def pack_far(step, tiles):
+        for s in range(2):
+            xy_out[step, s] = tiles[s]
+            for j, i in enumerate(CROSS_X[s]):
+                value = field[step, i, plane(PX if s else 1), :]
+                x_out[step, s, j] = value
+                cz = VELOCITIES[i][2]
+                if cz:
+                    at = side(-cz) * (PZ - 1)
+                    xz_out[step, s, pl.ds(at, 1), :] = value[at : at + 1, :]
+
+    def pack_near(step, tiles):
         for s in range(2):
             y_out[step, s] = tiles[s]
             for j, i in enumerate(CROSS_Z[s]):
                 z_out[step, s, j] = field[step, i, pl.ds(PZ + s * (PZ - 1), PX, stride=PZ), :]
-            for j, i in enumerate(CROSS_X[s]):
-                x_out[step, s, j] = field[step, i, pl.ds(PZ * (PX if s else 1), PZ), :]
-        if step == 0:
-            pl.semaphore_wait(barrier, len(ROUTES))
-        copies = {}
-        for k, route in enumerate(ROUTES):
-            dx, dy, dz = route
-            if route in FACES_X:
-                src, dst = x_out.at[step, side(dx)], x_in.at[step, side(dx)]
-            elif route in FACES_Z:
-                src, dst = z_out.at[step, side(dz)], z_in.at[step, side(dz)]
-            elif route in FACES_Y:
-                src, dst = y_out.at[step, side(dy)], y_in.at[step, side(dy)]
-            elif route in EDGES_XY:
-                src, dst = y_out.at[step, side(dy)], xy_in.at[step, side(dx), side(dy)]
-            elif route in EDGES_YZ:
-                src, dst = y_out.at[step, side(dy)], yz_in.at[step, side(dy), side(dz)]
-            else:
-                j = CROSS_Z[side(dz)].index(VELOCITIES.index((-dx, 0, -dz)))
-                src = z_out.at[step, side(dz), j, pl.ds(side(dx) * (PX - 8), 8), :]
-                dst = xz_in.at[step, side(dx), side(dz)]
-            copy = pltpu.make_async_remote_copy(
-                src_ref=src,
-                dst_ref=dst,
-                send_sem=send_sem.at[step, k],
-                recv_sem=recv_sem.at[step, k],
-                device_id=device(route),
-                device_id_type=pl.DeviceIdType.MESH,
-            )
-            copy.start()
-            copies[route] = copy
-        return copies
-
-    def insert_y(step, copies):
+
+    def send(step, routes):
+        for route in routes:
+            transfer(step, route).start()
+
+    def insert_y(step):
         for route in FACES_Y + EDGES_YZ:
-            copies[route].wait_recv()
+            transfer(step, route).wait_recv()
         tiles = {}
         for s in range(2):
             for i in CROSS_Y[s]:
@@ -231,14 +241,14 @@
         def body(x, carry):
             for s in range(2):
                 for j, i in enumerate(CROSS_Y[s]):
-                    put_column(step, i, x, tiles[i], x + j * PX)
+                    pull_y(step, i, x, tiles[i], x + j * PX)
             return carry
 
         lax.fori_loop(0, PX, body, 0, unroll=4)
 
-    def insert_z(step, copies):
+    def insert_z(step):
         for route in FACES_Z:
-            copies[route].wait_recv()
+            transfer(step, route).wait_recv()
         wide = lax.broadcasted_iota(jnp.int32, (PX, PY), 1)
         for s in range(2):
             for j, i in enumerate(CROSS_Z[s]):
@@ -246,14 +256,15 @@
                 value = z_in[step, s, j]
                 cy = VELOCITIES[i][1]
                 if cy:
+                    value = pltpu.roll(value, PY - 1 if cy == 1 else 1, axis=1)
                     value = jnp.where(
-                        wide == (0 if cy == 1 else PY - 1), field[step, i, rows, :], value
+                        wide == (PY - 1 if cy == 1 else 0), field[step, i, rows, :], value
                     )
                 field[step, i, rows, :] = value
 
-    def insert_x(step, copies):
+    def insert_x(step):
         for route in FACES_X + EDGES_XY + EDGES_XZ:
-            copies[route].wait_recv()
+            transfer(step, route).wait_recv()
         for s in range(2):
             for j, i in enumerate(CROSS_X[s]):
                 field[step, i, plane(0 if s else PX + 1), :] = x_in[step, s, j]
@@ -261,77 +272,81 @@
             i = VELOCITIES.index((-dx, 0, -dz))
             at = (0 if dx == 1 else PZ * (PX + 1)) + side(dz) * (PZ - 1)
             field[step, i, pl.ds(at, 1), :] = xz_in[
-                step, side(dx), side(dz), pl.ds(side(dx) * (PZ - 1), 1), :
+                step, side(dx), side(dz), pl.ds(side(dz) * (PZ - 1), 1), :
             ]
         for dx, dy, _ in EDGES_XY:
             i = VELOCITIES.index((-dx, -dy, 0))
             at = CROSS_Y[side(dy)].index(i) * PX + (PX - 1 if dx == 1 else 0)
-            put_column(step, i, -1 if dx == 1 else PX, xy_in[step, side(dx), side(dy)], at)
-
-    def advance(step, x):
+            pull_y(step, i, -1 if dx == 1 else PX, xy_in[step, side(dx), side(dy)], at)
+
+    def advance(old, new, x):
         pulled = []
         for i, (cx, cy, cz) in enumerate(VELOCITIES):
-            value = field[step, i, plane(x + (1 + cx)), :]
+            value = field[old, i, plane(x + (1 + cx)), :]
             if cz:
                 value = pltpu.roll(value, PZ - 1 if cz == 1 else 1, axis=0)
-            if cy:
-                value = pltpu.roll(value, PY - 1 if cy == 1 else 1, axis=1)
             pulled.append(value)
-        here_rows = plane(x)
-        u = [vel[d, here_rows, :] for d in range(3)]
-        new, gain = collide(
-            pulled, rho[here_rows, :], u, por[here_rows, :], node[here_rows, :]
-        )
-        sens[here_rows, :] = sens[here_rows, :] + gain
-        return new
-
-    def first_step(x, carry):
-        new = advance(0, x)
+        rows = plane(x)
+        u = [vel[d, rows, :] for d in range(3)]
+        made, gain = collide(pulled, rho[rows, :], u, por[rows, :], node[rows, :])
         for i in range(19):
-            field[1, i, plane(x + 1), :] = new[i]
+            field[new, i, plane(x + 1), :] = made[i]
+        sens[new, rows, :] = sens[old, rows, :] + gain
+
+    def one_step(step, carry):
+        def inner(x, c):
+            advance(step, step + 1, x)
+            return c
+
+        insert_y(step)
+        insert_z(step)
+        insert_x(step)
+        for x in (0, PX - 1):
+            advance(step, step + 1, x)
+
+        @pl.when(step == 0)
+        def _():
+            tiles = (blank,) * 2
+            for x in (0, PX - 1):
+                tiles = pack_columns(1, x, tiles)
+            pack_far(1, tiles)
+            send(1, FAR)
+
+        lax.fori_loop(1, PX - 1, inner, 0, unroll=2)
+
+        @pl.when(step == 0)
+        def _():
+            tiles = (xy_out[1, 0], xy_out[1, 1])
+            for x in range(1, PX - 1):
+                tiles = pack_columns(1, x, tiles)
+            pack_near(1, tiles)
+            send(1, NEAR)
+
         return carry
 
-    def second_step(x, carry):
-        new = advance(1, x)
-        for i in range(19):
-            result[i, plane(x), :] = new[i]
-        return carry
-
-    def pack(step, low, high, tiles):
-        return lax.fori_loop(
-            low, high, lambda x, t: pack_columns(step, x, t), tiles, unroll=high - low
-        )
-
-    blank = (jnp.zeros((PZ, PY), jnp.float32),) * 2
+    blank = jnp.zeros((PZ, PY), jnp.float32)
     loads[0].wait()
-    tiles = pack(0, 0, PX, blank)
-    first = exchange(0, tiles)
+    tiles = (blank,) * 2
+    for x in range(PX):
+        tiles = pack_columns(0, x, tiles)
+    pack_far(0, tiles)
+    pack_near(0, tiles)
+    pl.semaphore_wait(barrier, len(ROUTES))
+    send(0, FAR[:8])
+    send(0, NEAR)
+    send(0, FAR[8:])
     for copy in loads[1:]:
         copy.wait()
-    insert_y(0, first)
-    insert_z(0, first)
-    lax.fori_loop(1, PX - 1, first_step, 0, unroll=7)
-    tiles = pack(1, 1, PX - 1, blank)
-    insert_x(0, first)
-    for x in (0, PX - 1):
-        first_step(x, 0)
-        tiles = pack_columns(1, x, tiles)
-    second = exchange(1, tiles)
-    insert_y(1, second)
-    insert_z(1, second)
-    lax.fori_loop(1, PX - 1, second_step, 0, unroll=7)
-    insert_x(1, second)
-    for x in (0, PX - 1):
-        second_step(x, 0)
-    for copies in (first, second):
+    lax.fori_loop(0, 2, one_step, 0)
+    for step in range(2):
         for route in ROUTES:
-            copies[route].wait_send()
-
-
-def store_kernel(result, sens, out_hbm, out_sens_hbm, sem):
+            transfer(step, route).wait_send()
+
+
+def store_kernel(field, sens, out_hbm, out_sens_hbm, sem):
     copies = [
-        pltpu.make_async_copy(result, out_hbm, sem.at[0]),
-        pltpu.make_async_copy(sens, out_sens_hbm, sem.at[1]),
+        pltpu.make_async_copy(field.at[2, :, pl.ds(PZ, ROWS), :], out_hbm, sem.at[0]),
+        pltpu.make_async_copy(sens.at[2], out_sens_hbm, sem.at[1]),
     ]
     for copy in copies:
         copy.start()
@@ -346,13 +361,12 @@
     made = pl.pallas_call(
         lattice_kernel,
         out_shape=(
-            pltpu.VMEM((19, ROWS, PY), f32),
-            pltpu.VMEM((ROWS, PY), f32),
+            pltpu.VMEM((3, 19, ROWS + 2 * PZ, PY), f32),
+            pltpu.VMEM((3, ROWS, PY), f32),
         ),
         in_specs=[anywhere] * 6,
         out_specs=(pl.BlockSpec(memory_space=pltpu.VMEM),) * 2,
         scratch_shapes=[
-            pltpu.VMEM((2, 19, ROWS + 2 * PZ, PY), f32),
             pltpu.VMEM((ROWS, PY), f32),
             pltpu.VMEM((3, ROWS, PY), f32),
             pltpu.VMEM((ROWS, PY), f32),
@@ -360,6 +374,8 @@
             pltpu.VMEM((2, 2, 5, PZ, PY), f32),
             pltpu.VMEM((2, 2, PZ, PY), f32),
             pltpu.VMEM((2, 2, 5, PX, PY), f32),
+            pltpu.VMEM((2, 2, PZ, PY), f32),
+            pltpu.VMEM((2, 2, PZ, PY), f32),
             pltpu.VMEM((2, 2, 5, PZ, PY), f32),
             pltpu.VMEM((2, 2, PZ, PY), f32),
             pltpu.VMEM((2, 2, 5, PX, PY), f32),

time: 30 us -> 29.3 us (0.977)
  Pallas kernels: 29.3 us -> 28.6 us
    pallas_call x1, Pallas kernels: 28.2 us -> 27.5 us  [shards(): pl.pallas_call(lattice_kernel, out_shape=(pltpu.VMEM((3, 19, ROWS + 2 * P...]
where the time goes in v3:
time: 29.3 us; the launch traced here: 29.2 us
  Pallas kernels  28.6 us (98%)
  between operations  0.64 us (2%)
    pallas_call x1, Pallas kernels, shards(): pl.pallas_call(lattice_kernel, out_shape=(pltpu.VMEM((3, 19, ROWS + 2 * P...  27.5 us
    pallas_call x1, Pallas kernels, shards(): pl.pallas_call(store_kernel, out_shape=(jax.ShapeDtypeStruct((19, ROWS, P...  1.06 us

profile of v3, /device:TPU:1, one launch (start us, length us, event | category | flops | bytes accessed | tf_op | source)
XLA Modules:
  0.0 29.2 jit_solution(18427781164121757495)
XLA Ops:
  0.6 27.5 %shard_map.77 = (f32[3,19,144,128]{3,2,1,0:T(8,128)S(1)}, f32[3,128,128]{2,1,0:T(8,128)S(1)}) custom-call(f32[19,128,128]{2,1,0:T(8,128)} %bitcast.8, f32[128,128]{1,0:T(8,128)} %bitcast.10, f32[3,128,128]{2,1,0:T(8,128)} %bitcast.9, f32[128,128]{1,0:T(8,128)} %bitcast.11, s32[128,128]{1,0:T(8,128)} %bitcast.12, f32[128,128]{1,0:T(8,128)} %bitcast.13), custom_call_target="tpu_custom_call" | custom-call | tf_op jit(solution)/shard_map/pallas_call | solution.py:361
  28.2 1.1 %shard_map.78 = (f32[19,128,128]{2,1,0:T(8,128)}, f32[128,128]{1,0:T(8,128)}) custom-call(f32[3,19,144,128]{3,2,1,0:T(8,128)S(1)} %get-tuple-element.6.field, f32[3,128,128]{2,1,0:T(8,128)S(1)} %get-tuple-element.7.sens), custom_call_target="tpu_custom_call" | custom-call | tf_op jit(solution)/shard_map/pallas_call | solution.py:400

commit v4 on v3

v4 whole, which is shorter than its diff:
```python
import functools

import jax
import jax.numpy as jnp
from jax import lax
from jax.experimental import pallas as pl
from jax.experimental.pallas import tpu as pltpu
from jax.sharding import PartitionSpec as P

AXES = ("gx", "gy", "gz")
PX, PZ, PY = 16, 8, 128
ROWS = PX * PZ

VELOCITIES = [
    (0, 0, 0),
    (1, 0, 0),
    (-1, 0, 0),
    (0, 1, 0),
    (0, -1, 0),
    (0, 0, 1),
    (0, 0, -1),
    (1, 1, 0),
    (-1, -1, 0),
    (1, -1, 0),
    (-1, 1, 0),
    (1, 0, 1),
    (-1, 0, -1),
    (1, 0, -1),
    (-1, 0, 1),
    (0, 1, 1),
    (0, -1, -1),
    (0, 1, -1),
    (0, -1, 1),
]
CROSS = [[[i for i, c in enumerate(VELOCITIES) if c[a] == s] for s in (1, -1)] for a in range(3)]
CROSS_X, CROSS_Y, CROSS_Z = CROSS
FACES_X = [(-1, 0, 0), (1, 0, 0)]
FACES_Y = [(0, -1, 0), (0, 1, 0)]
FACES_Z = [(0, 0, -1), (0, 0, 1)]
EDGES_XY = [(a, b, 0) for a in (-1, 1) for b in (-1, 1)]
EDGES_YZ = [(0, a, b) for a in (-1, 1) for b in (-1, 1)]
EDGES_XZ = [(a, 0, b) for a in (-1, 1) for b in (-1, 1)]
FAR = EDGES_XZ + EDGES_XY + FACES_X
NEAR = EDGES_YZ + FACES_Y
ROUTES = FAR + FACES_Z + NEAR
CORNERS = EDGES_XZ + EDGES_XY
GROUP_FAR, GROUP_Z, GROUP_NEAR = 0, 1, 3


def side(sign):
    return (sign + 1) // 2


def collide(p, rho, u, g, node):
    ux, uy, uz = u
    e = [p[i] + p[i + 1] for i in range(1, 19, 2)]
    o = [p[i] - p[i + 1] for i in range(1, 19, 2)]
    sxy, sxz, syz = e[3] + e[4], e[5] + e[6], e[7] + e[8]
    dxy, dxz, dyz = e[3] - e[4], e[5] - e[6], e[7] - e[8]
    sx = 2.0 * e[0] + (sxy + sxz)
    sy = 2.0 * e[1] + (sxy + syz)
    sz = 2.0 * e[2] + (sxz + syz)
    trace = sx + sy + sz
    h36 = 12.0 * p[0] + (trace - (sxy + sxz + syz))
    third = h36 * (1.0 / 3.0)
    mxx, myy, mzz = sx - third, sy - third, sz - third
    hcx = 2.0 * o[0] + ((o[3] + o[4]) + (o[5] + o[6]))
    hcy = 2.0 * o[1] + ((o[3] - o[4]) + (o[7] + o[8]))
    hcz = 2.0 * o[2] + ((o[5] - o[6]) + (o[7] - o[8]))
    nx = mxx * ux + dxy * uy + dxz * uz
    ny = dxy * ux + myy * uy + dyz * uz
    nz = dxz * ux + dyz * uy + mzz * uz
    q = ux * nx + uy * ny + uz * nz
    first = ux * hcx + uy * hcy + uz * hcz
    g4 = 0.4 * g
    b = g4 * g
    a = g * (1.0 / 12.0) + (1.0 / 60.0)
    gain = rho * (first * (1.0 / 12.0) + g4 * q)
    inlet = node == 1
    wall = node == 2
    vx = a * hcx + b * nx + jnp.where(inlet, 1.0, 0.0)
    vy = a * hcy + b * ny
    vz = a * hcz + b * nz
    base = h36 * (1.1 / 36.0) + trace * (1.0 / 120.0) - (0.5 * b) * q
    ex, ey, ez = -0.025 * mxx, -0.025 * myy, -0.025 * mzz
    bx, by = base + ex, base + ey
    bz = base + ez
    bxy, bxz, byz = bx + ey, bx + ez, by + ez
    wxy, wxz, wyz = 0.05 * dxy, 0.05 * dxz, 0.05 * dyz
    even = [bx, by, bz, bxy - wxy, bxy + wxy, bxz - wxz, bxz + wxz, byz - wyz, byz + wyz]
    odd = [vx, vy, vz, vx + vy, vx - vy, vx + vz, vx - vz, vy + vz, vy - vz]
    new = [jnp.where(wall, p[0], base - 0.4 * p[0])]
    for k in range(9):
        up = even[k] - 0.2 * e[k]
        down = odd[k] - 0.1 * o[k]
        new.append(jnp.where(wall, p[2 * k + 2], up + down))
        new.append(jnp.where(wall, p[2 * k + 1], up - down))
    return new, jnp.where(wall, 0.0, gain)


def plane(x):
    if isinstance(x, int):
        return pl.ds(x * PZ, PZ)
    return pl.ds(pl.multiple_of(x * PZ, PZ), PZ)


def advance(old, rows, rho, vel, por, node):
    pulled = []
    for value, (_, _, cz) in zip(old, VELOCITIES):
        if cz:
            value = pltpu.roll(value, PZ - 1 if cz == 1 else 1, axis=0)
        pulled.append(value)
    u = [vel[d, rows, :] for d in range(3)]
    return collide(pulled, rho[rows, :], u, por[rows, :], node[rows, :])


def lattice_kernel(
    adj_hbm,
    rho_hbm,
    vel_hbm,
    por_hbm,
    node_hbm,
    sens_hbm,
    field,
    sens,
    rho,
    vel,
    por,
    node,
    x_out,
    y_out,
    z_out,
    xy_out,
    xz_out,
    far_in,
    near_in,
    z_in,
    load_sem,
    send_sem,
    recv_sem,
):
    here = [lax.axis_index(a) for a in AXES]
    size = [lax.axis_size(a) for a in AXES]

    def device(route):
        return tuple(lax.rem(h + (d + n), n) if d else h for h, d, n in zip(here, route, size))

    barrier = pltpu.get_barrier_semaphore()
    for route in ROUTES:
        pl.semaphore_signal(
            barrier, inc=1, device_id=device(route), device_id_type=pl.DeviceIdType.MESH
        )
    own = pl.ds(PZ, ROWS)
    loads = [
        pltpu.make_async_copy(src, dst, load_sem.at[k])
        for k, (src, dst) in enumerate(
            [
                (adj_hbm, field.at[0, :, own, :]),
                (rho_hbm, rho),
                (vel_hbm, vel),
                (por_hbm, por),
                (node_hbm, node),
                (sens_hbm, sens.at[0]),
            ]
        )
    ]
    for copy in loads:
        copy.start()

    lane = lax.broadcasted_iota(jnp.int32, (PZ, PY), 1)
    row = lax.broadcasted_iota(jnp.int32, (PZ, PY), 0)

    def pack_columns(step, x, tiles):
        made = []
        for s in range(2):
            tile = tiles[s]
            for j, i in enumerate(CROSS_Y[s]):
                at = x + j * PX
                value = field[step, i, plane(x + 1), :]
                turned = pltpu.roll(value, at if s == 0 else at + 1, axis=1)
                tile = jnp.where(lane == at, turned, tile)
            made.append(tile)
        return tuple(made)

    def pull_y(step, i, x, tile, at):
        cy = VELOCITIES[i][1]
        edge = PY - 1 if cy == 1 else 0
        shift = (edge - at) % PY if isinstance(at, int) else (edge or PY) - at
        column = pltpu.roll(tile, shift, axis=1)
        value = pltpu.roll(field[step, i, plane(x + 1), :], PY - 1 if cy == 1 else 1, axis=1)
        field[step, i, plane(x + 1), :] = jnp.where(lane == edge, column, value)

    def x_part(buffer, step, s):
        return buffer.at[step, pl.ds(len(CORNERS) + 5 * s, 5)]

    def copy_of(step, group, src, dst, route):
        return pltpu.make_async_remote_copy(
            src_ref=src,
            dst_ref=dst,
            send_sem=send_sem.at[step, group],
            recv_sem=recv_sem.at[step, group],
            device_id=device(route),
            device_id_type=pl.DeviceIdType.MESH,
        )

    def transfer(step, route, half=0):
        dx, dy, dz = route
        if route in FACES_X:
            src, dst = x_out.at[step, side(dx)], x_part(far_in, step, side(dx))
        elif route in FACES_Z:
            src, dst = z_out.at[step, half, side(dz)], z_in.at[step, half, side(dz)]
        elif route in NEAR:
            src, dst = y_out.at[step, side(dy)], near_in.at[step, NEAR.index(route)]
        elif route in EDGES_XY:
            src, dst = xy_out.at[step, side(dy)], far_in.at[step, CORNERS.index(route)]
        else:
            src, dst = xz_out.at[step, side(dx)], far_in.at[step, CORNERS.index(route)]
        if route in FACES_Z:
            return copy_of(step, GROUP_Z + half, src, dst, route)
        return copy_of(step, GROUP_NEAR if route in NEAR else GROUP_FAR, src, dst, route)

    def whole(step, group):
        if group == GROUP_FAR:
            buffer = far_in.at[step]
        elif group == GROUP_NEAR:
            buffer = near_in.at[step]
        else:
            buffer = z_in.at[step, group - GROUP_Z]
        return copy_of(step, group, buffer, buffer, FACES_X[0])

    def pack_xz(step):
        for s in range(2):
            for i in CROSS_X[s]:
                cz = VELOCITIES[i][2]
                if cz:
                    at = side(-cz) * (PZ - 1)
                    line = pl.ds(PZ * (PX if s else 1) + at, 1)
                    xz_out[step, s, pl.ds(at, 1), :] = field[step, i, line, :]

    def pack_x(step, tiles):
        for s in range(2):
            xy_out[step, s] = tiles[s]
            for j, i in enumerate(CROSS_X[s]):
                x_out[step, s, j] = field[step, i, plane(PX if s else 1), :]

    def z_rows(s, half):
        return pl.ds(PZ + s * (PZ - 1) + half * (ROWS // 2), PX // 2, stride=PZ)

    def pack_z(step, half):
        for s in range(2):
            for j, i in enumerate(CROSS_Z[s]):
                z_out[step, half, s, j] = field[step, i, z_rows(s, half), :]

    def send_z(step, half):
        for route in FACES_Z:
            transfer(step, route, half).start()

    def pack_near(step, tiles):
        for s in range(2):
            y_out[step, s] = tiles[s]

    def send(step, routes):
        for route in routes:
            transfer(step, route).start()

    def insert_y(step):
        whole(step, GROUP_NEAR).wait_recv()
        tiles = {}
        for s in range(2):
            for i in CROSS_Y[s]:
                cz = VELOCITIES[i][2]
                tiles[i] = near_in[step, NEAR.index(FACES_Y[s])]
                if cz:
                    corner = near_in[step, NEAR.index((0, 2 * s - 1, -cz))]
                    tiles[i] = jnp.where(row == (0 if cz == 1 else PZ - 1), corner, tiles[i])

        def body(x, carry):
            for s in range(2):
                for j, i in enumerate(CROSS_Y[s]):
                    pull_y(step, i, x, tiles[i], x + j * PX)
            return carry

        lax.fori_loop(0, PX, body, 0, unroll=4)

    def insert_z(step, half):
        whole(step, GROUP_Z + half).wait_recv()
        for s in range(2):
            for j, i in enumerate(CROSS_Z[s]):
                rows = z_rows(s, half)
                value = z_in[step, half, s, j]
                cy = VELOCITIES[i][1]
                if cy:
                    value = pltpu.roll(value, PY - 1 if cy == 1 else 1, axis=1)
                    value = jnp.where(
                        lane == (PY - 1 if cy == 1 else 0), field[step, i, rows, :], value
                    )
                field[step, i, rows, :] = value

    def insert_x(step):
        whole(step, GROUP_FAR).wait_recv()
        for s in range(2):
            for j, i in enumerate(CROSS_X[s]):
                field[step, i, plane(0 if s else PX + 1), :] = far_in[
                    step, len(CORNERS) + 5 * s + j
                ]
        for route in EDGES_XZ:
            dx, _, dz = route
            i = VELOCITIES.index((-dx, 0, -dz))
            at = side(dz) * (PZ - 1)
            field[step, i, pl.ds((0 if dx == 1 else PZ * (PX + 1)) + at, 1), :] = far_in[
                step, CORNERS.index(route), pl.ds(at, 1), :
            ]
        for route in EDGES_XY:
            dx, dy, _ = route
            i = VELOCITIES.index((-dx, -dy, 0))
            at = CROSS_Y[side(dy)].index(i) * PX + (PX - 1 if dx == 1 else 0)
            tile = far_in[step, CORNERS.index(route)]
            pull_y(step, i, -1 if dx == 1 else PX, tile, at)

    def step_plane(step, x):
        old = [field[step, i, plane(x + 1 + c[0]), :] for i, c in enumerate(VELOCITIES)]
        rows = plane(x)
        new, gain = advance(old, rows, rho, vel, por, node)
        for i in range(19):
            field[step + 1, i, plane(x + 1), :] = new[i]
        sens[step + 1, rows, :] = sens[step, rows, :] + gain

    def one_step(step, carry):
        def pair(k, c):
            step_plane(step, 2 * k + 1)
            step_plane(step, 2 * k + 2)
            return c

        def part(half, c):
            @pl.when(jnp.logical_and(step == 1, half == 1))
            def _():
                insert_z(1, 1)

            lax.fori_loop(3 * half, 3 + 4 * half, pair, 0)

            @pl.when(jnp.logical_and(step == 0, half == 0))
            def _():
                pack_z(1, 0)
                send_z(1, 0)

            return c

        insert_y(step)
        insert_z(step, 0)

        @pl.when(step == 0)
        def _():
            insert_z(0, 1)
            insert_x(0)
            for x in (0, PX - 1):
                step_plane(0, x)
            pack_xz(1)
            send(1, EDGES_XZ)
            step_plane(0, PX // 2 - 1)
            tiles = (blank,) * 2
            for x in (0, PX - 1):
                tiles = pack_columns(1, x, tiles)
            pack_x(1, tiles)
            send(1, EDGES_XY + FACES_X)

        lax.fori_loop(0, 2, part, 0)

        @pl.when(step == 0)
        def _():
            pack_z(1, 1)
            send_z(1, 1)
            tiles = (xy_out[1, 0], xy_out[1, 1])
            for x in range(1, PX - 1):
                tiles = pack_columns(1, x, tiles)
            pack_near(1, tiles)
            send(1, NEAR)
            for group in range(4):
                whole(0, group).wait_send()

        return carry

    blank = jnp.zeros((PZ, PY), jnp.float32)
    loads[0].wait()
    tiles = (blank,) * 2
    for x in range(PX):
        tiles = pack_columns(0, x, tiles)
    pack_xz(0)
    pack_x(0, tiles)
    pack_near(0, tiles)
    pack_z(0, 0)
    pack_z(0, 1)
    pl.semaphore_wait(barrier, len(ROUTES))
    send(0, EDGES_XZ)
    send_z(0, 0)
    send_z(0, 1)
    send(0, EDGES_XY + FACES_X + NEAR)
    for copy in loads[1:]:
        copy.wait()
    lax.fori_loop(0, 2, one_step, 0)
    insert_x(1)
    for group in range(4):
        whole(1, group).wait_send()


def last_kernel(field, sens, rho, vel, por, node, out_hbm, out_sens_hbm, result, gained, sem):
    inner = pl.ds(PZ, ROWS - 2 * PZ)
    copies = [
        pltpu.make_async_copy(
            field.at[2, :, pl.ds(2 * PZ, ROWS - 2 * PZ), :], out_hbm.at[:, inner, :], sem.at[0]
        ),
        pltpu.make_async_copy(sens.at[2, inner, :], out_sens_hbm.at[inner, :], sem.at[1]),
    ]
    for copy in copies:
        copy.start()
    for k, x in enumerate((0, PX - 1)):
        old = [field[1, i, plane(x + 1 + c[0]), :] for i, c in enumerate(VELOCITIES)]
        rows = plane(x)
        new, gain = advance(old, rows, rho, vel, por, node)
        for i in range(19):
            result[k, i] = new[i]
        gained[k] = sens[1, rows, :] + gain
    for k, x in enumerate((0, PX - 1)):
        rows = plane(x)
        copies.append(
            pltpu.make_async_copy(result.at[k], out_hbm.at[:, rows, :], sem.at[2 + 2 * k])
        )
        copies.append(
            pltpu.make_async_copy(gained.at[k], out_sens_hbm.at[rows, :], sem.at[3 + 2 * k])
        )
    for copy in copies[2:]:
        copy.start()
    for copy in copies:
        copy.wait()


def shards(adjoint, density, velocity, porosity, node_type, sensitivity_in):
    f32 = jnp.float32
    dma = pltpu.SemaphoreType.DMA
    anywhere = pl.BlockSpec(memory_space=pl.ANY)
    vmem = pl.BlockSpec(memory_space=pltpu.VMEM)
    made = pl.pallas_call(
        lattice_kernel,
        out_shape=(
            pltpu.VMEM((3, 19, ROWS + 2 * PZ, PY), f32),
            pltpu.VMEM((3, ROWS, PY), f32),
            pltpu.VMEM((ROWS, PY), f32),
            pltpu.VMEM((3, ROWS, PY), f32),
            pltpu.VMEM((ROWS, PY), f32),
            pltpu.VMEM((ROWS, PY), jnp.int32),
        ),
        in_specs=[anywhere] * 6,
        out_specs=(vmem,) * 6,
        scratch_shapes=[
            pltpu.VMEM((2, 2, 5, PZ, PY), f32),
            pltpu.VMEM((2, 2, PZ, PY), f32),
            pltpu.VMEM((2, 2, 2, 5, PX // 2, PY), f32),
            pltpu.VMEM((2, 2, PZ, PY), f32),
            pltpu.VMEM((2, 2, PZ, PY), f32),
            pltpu.VMEM((2, len(CORNERS) + 10, PZ, PY), f32),
            pltpu.VMEM((2, len(NEAR), PZ, PY), f32),
            pltpu.VMEM((2, 2, 2, 5, PX // 2, PY), f32),
            dma((6,)),
            dma((2, 4)),
            dma((2, 4)),
        ],
        compiler_params=pltpu.CompilerParams(
            collective_id=0, has_side_effects=True, vmem_limit_bytes=56 * 1024 * 1024
        ),
    )(
        adjoint.reshape(19, ROWS, PY),
        density.reshape(ROWS, PY),
        velocity.reshape(3, ROWS, PY),
        porosity.reshape(ROWS, PY),
        node_type.reshape(ROWS, PY),
        sensitivity_in.reshape(ROWS, PY),
    )
    out, sens = pl.pallas_call(
        last_kernel,
        out_shape=(
            jax.ShapeDtypeStruct((19, ROWS, PY), f32),
            jax.ShapeDtypeStruct((ROWS, PY), f32),
        ),
        in_specs=[vmem] * 6,
        out_specs=(anywhere, anywhere),
        scratch_shapes=[
            pltpu.VMEM((2, 19, PZ, PY), f32),
            pltpu.VMEM((2, PZ, PY), f32),
            dma((6,)),
        ],
        compiler_params=pltpu.CompilerParams(vmem_limit_bytes=8 * 1024 * 1024),
    )(*made)
    return out.reshape(19, PX, PZ, PY), sens.reshape(PX, PZ, PY)


def solution(mesh):
    cells = P("gx", "gz", "gy")
    many = P(None, "gx", "gz", "gy")
    return jax.shard_map(
        shards,
        mesh=mesh,
        in_specs=(many, cells, many, cells, cells, cells),
        out_specs=(many, cells),
        check_vma=False,
    )
```

time: 29.3 us -> 28.3 us (0.966)
  Pallas kernels: 28.6 us -> 27.6 us
    pallas_call x1, Pallas kernels: 27.5 us -> 26.5 us  [shards(): pl.pallas_call(lattice_kernel, out_shape=(pltpu.VMEM((3, 19, ROWS + 2 * P...]
where the time goes in v4:
time: 28.3 us; the launch traced here: 28.2 us
  Pallas kernels  27.6 us (98%)
  between operations  0.64 us (2%)
    pallas_call x1, Pallas kernels, shards(): pl.pallas_call(lattice_kernel, out_shape=(pltpu.VMEM((3, 19, ROWS + 2 * P...  26.5 us
    pallas_call x1, Pallas kernels, shards(): pl.pallas_call(last_kernel, out_shape=(jax.ShapeDtypeStruct((19, ROWS, PY...  1.1 us

profile of v4, /device:TPU:1, one launch (start us, length us, event | category | flops | bytes accessed | tf_op | source)
XLA Modules:
  0.0 28.2 jit_solution(17740296688751739283)
XLA Ops:
  0.6 26.5 %shard_map.77 = (f32[3,19,144,128]{3,2,1,0:T(8,128)S(1)}, f32[3,128,128]{2,1,0:T(8,128)S(1)}, f32[128,128]{1,0:T(8,128)S(1)}, f32[3,128,128]{2,1,0:T(8,128)S(1)}...) custom-call(f32[19,128,128]{2,1,0:T(8,128)} %bitcast.8, f32[128,128]{1,0:T(8,128)} %bitcast.10, f32[3,128,128]{2,1,0:T(8,128)} %bitcast.9, ...), custom_call_target="tpu_custom_call" | custom-call | tf_op jit(solution)/shard_map/pallas_call | solution.py:441
  27.1 1.1 %shard_map.78 = (f32[19,128,128]{2,1,0:T(8,128)}, f32[128,128]{1,0:T(8,128)}) custom-call(f32[3,19,144,128]{3,2,1,0:T(8,128)S(1)} %get-tuple-element.10.field, f32[3,128,128]{2,1,0:T(8,128)S(1)} %get-tuple-element.11.sens, f32[128,128]{1,0:T(8,128)S(1)} %get-tuple-element.12.rho, f32[3,128,128]{2,1,0:T(8,128)S(1)} %get-tuple-element.13.vel, ...), custom_call_target="tpu_custom_call" | custom-call | tf_op jit(solution)/shard_map/pallas_call | solution.py:477

commit v5 on v4

--- a/solution.py
+++ b/solution.py
@@ -44,7 +44,8 @@
 NEAR = EDGES_YZ + FACES_Y
 ROUTES = FAR + FACES_Z + NEAR
 CORNERS = EDGES_XZ + EDGES_XY
-GROUP_FAR, GROUP_Z, GROUP_NEAR = 0, 1, 3
+GROUP_FAR, GROUP_Z, GROUP_NEAR, GROUP_RELAY = 0, 1, 3, 4
+GREETED = FACES_X + FACES_Z + NEAR
 
 
 def side(sign):
@@ -135,6 +136,7 @@
     far_in,
     near_in,
     z_in,
+    relay_in,
     load_sem,
     send_sem,
     recv_sem,
@@ -146,7 +148,7 @@
         return tuple(lax.rem(h + (d + n), n) if d else h for h, d, n in zip(here, route, size))
 
     barrier = pltpu.get_barrier_semaphore()
-    for route in ROUTES:
+    for route in GREETED:
         pl.semaphore_signal(
             barrier, inc=1, device_id=device(route), device_id_type=pl.DeviceIdType.MESH
         )
@@ -214,7 +216,7 @@
         elif route in EDGES_XY:
             src, dst = xy_out.at[step, side(dy)], far_in.at[step, CORNERS.index(route)]
         else:
-            src, dst = xz_out.at[step, side(dx)], far_in.at[step, CORNERS.index(route)]
+            src, dst = xz_out.at[step, side(dz)], far_in.at[step, CORNERS.index(route)]
         if route in FACES_Z:
             return copy_of(step, GROUP_Z + half, src, dst, route)
         return copy_of(step, GROUP_NEAR if route in NEAR else GROUP_FAR, src, dst, route)
@@ -224,18 +226,37 @@
             buffer = far_in.at[step]
         elif group == GROUP_NEAR:
             buffer = near_in.at[step]
+        elif group == GROUP_RELAY:
+            buffer = relay_in
         else:
             buffer = z_in.at[step, group - GROUP_Z]
         return copy_of(step, group, buffer, buffer, FACES_X[0])
 
     def pack_xz(step):
         for s in range(2):
-            for i in CROSS_X[s]:
-                cz = VELOCITIES[i][2]
-                if cz:
-                    at = side(-cz) * (PZ - 1)
-                    line = pl.ds(PZ * (PX if s else 1) + at, 1)
-                    xz_out[step, s, pl.ds(at, 1), :] = field[step, i, line, :]
+            for i in CROSS_Z[s]:
+                cx = VELOCITIES[i][0]
+                if cx:
+                    line = pl.ds(PZ * (1 if cx == 1 else PX) + s * (PZ - 1), 1)
+                    xz_out[step, s, pl.ds(side(-cx) * (PZ - 1), 1), :] = field[step, i, line, :]
+
+    def send_corner_rows():
+        for s, route in enumerate(FACES_Z):
+            copy_of(0, GROUP_RELAY, xz_out.at[0, s], relay_in.at[s], route).start()
+
+    def relay():
+        def forward(src, dx, dy, dz):
+            dst = far_in.at[0, CORNERS.index((dx, dy, dz))]
+            copy_of(0, GROUP_FAR, src, dst, (dx, 0, 0)).start()
+
+        whole(0, GROUP_RELAY).wait_recv()
+        for dx in (-1, 1):
+            for dz in (-1, 1):
+                forward(relay_in.at[side(dz)], dx, 0, dz)
+        whole(0, GROUP_NEAR).wait_recv()
+        for dx in (-1, 1):
+            for dy in (-1, 1):
+                forward(near_in.at[0, NEAR.index((0, dy, 0))], dx, dy, 0)
 
     def pack_x(step, tiles):
         for s in range(2):
@@ -264,7 +285,10 @@
             transfer(step, route).start()
 
     def insert_y(step):
-        whole(step, GROUP_NEAR).wait_recv()
+        @pl.when(step == 1)
+        def _():
+            whole(1, GROUP_NEAR).wait_recv()
+
         tiles = {}
         for s in range(2):
             for i in CROSS_Y[s]:
@@ -308,7 +332,7 @@
             i = VELOCITIES.index((-dx, 0, -dz))
             at = side(dz) * (PZ - 1)
             field[step, i, pl.ds((0 if dx == 1 else PZ * (PX + 1)) + at, 1), :] = far_in[
-                step, CORNERS.index(route), pl.ds(at, 1), :
+                step, CORNERS.index(route), pl.ds(side(dx) * (PZ - 1), 1), :
             ]
         for route in EDGES_XY:
             dx, dy, _ = route
@@ -374,7 +398,7 @@
                 tiles = pack_columns(1, x, tiles)
             pack_near(1, tiles)
             send(1, NEAR)
-            for group in range(4):
+            for group in range(5):
                 whole(0, group).wait_send()
 
         return carry
@@ -389,13 +413,15 @@
     pack_near(0, tiles)
     pack_z(0, 0)
     pack_z(0, 1)
-    pl.semaphore_wait(barrier, len(ROUTES))
-    send(0, EDGES_XZ)
+    pl.semaphore_wait(barrier, len(GREETED))
+    send_corner_rows()
+    send(0, NEAR)
     send_z(0, 0)
     send_z(0, 1)
-    send(0, EDGES_XY + FACES_X + NEAR)
+    send(0, FACES_X)
     for copy in loads[1:]:
         copy.wait()
+    relay()
     lax.fori_loop(0, 2, one_step, 0)
     insert_x(1)
     for group in range(4):
@@ -459,9 +485,10 @@
             pltpu.VMEM((2, len(CORNERS) + 10, PZ, PY), f32),
             pltpu.VMEM((2, len(NEAR), PZ, PY), f32),
             pltpu.VMEM((2, 2, 2, 5, PX // 2, PY), f32),
+            pltpu.VMEM((2, PZ, PY), f32),
             dma((6,)),
-            dma((2, 4)),
-            dma((2, 4)),
+            dma((2, 5)),
+            dma((2, 5)),
         ],
         compiler_params=pltpu.CompilerParams(
             collective_id=0, has_side_effects=True, vmem_limit_bytes=56 * 1024 * 1024

time: 28.3 us -> 28 us (0.989)
  Pallas kernels: 27.6 us -> 27.3 us
    pallas_call x1, Pallas kernels: 26.5 us -> 26.2 us  [shards(): pl.pallas_call(lattice_kernel, out_shape=(pltpu.VMEM((3, 19, ROWS + 2 * P...]
where the time goes in v5:
time: 28 us; the launch traced here: 27.9 us
  Pallas kernels  27.3 us (98%)
  between operations  0.64 us (2%)
    pallas_call x1, Pallas kernels, shards(): pl.pallas_call(lattice_kernel, out_shape=(pltpu.VMEM((3, 19, ROWS + 2 * P...  26.2 us
    pallas_call x1, Pallas kernels, shards(): pl.pallas_call(last_kernel, out_shape=(jax.ShapeDtypeStruct((19, ROWS, PY...  1.1 us

profile of v5, /device:TPU:1, one launch (start us, length us, event | category | flops | bytes accessed | tf_op | source)
XLA Modules:
  0.0 27.9 jit_solution(4278901801138935626)
XLA Ops:
  0.6 26.2 %shard_map.77 = (f32[3,19,144,128]{3,2,1,0:T(8,128)S(1)}, f32[3,128,128]{2,1,0:T(8,128)S(1)}, f32[128,128]{1,0:T(8,128)S(1)}, f32[3,128,128]{2,1,0:T(8,128)S(1)}...) custom-call(f32[19,128,128]{2,1,0:T(8,128)} %bitcast.8, f32[128,128]{1,0:T(8,128)} %bitcast.10, f32[3,128,128]{2,1,0:T(8,128)} %bitcast.9, ...), custom_call_target="tpu_custom_call" | custom-call | tf_op jit(solution)/shard_map/pallas_call | solution.py:467
  26.8 1.1 %shard_map.78 = (f32[19,128,128]{2,1,0:T(8,128)}, f32[128,128]{1,0:T(8,128)}) custom-call(f32[3,19,144,128]{3,2,1,0:T(8,128)S(1)} %get-tuple-element.10.field, f32[3,128,128]{2,1,0:T(8,128)S(1)} %get-tuple-element.11.sens, f32[128,128]{1,0:T(8,128)S(1)} %get-tuple-element.12.rho, f32[3,128,128]{2,1,0:T(8,128)S(1)} %get-tuple-element.13.vel, ...), custom_call_target="tpu_custom_call" | custom-call | tf_op jit(solution)/shard_map/pallas_call | solution.py:504

commit v6 on v5

--- a/solution.py
+++ b/solution.py
@@ -128,12 +128,12 @@
     vel,
     por,
     node,
+    far_in,
     x_out,
     y_out,
     z_out,
     xy_out,
     xz_out,
-    far_in,
     near_in,
     z_in,
     relay_in,
@@ -355,47 +355,29 @@
             step_plane(step, 2 * k + 2)
             return c
 
-        def part(half, c):
-            @pl.when(jnp.logical_and(step == 1, half == 1))
-            def _():
-                insert_z(1, 1)
-
-            lax.fori_loop(3 * half, 3 + 4 * half, pair, 0)
-
-            @pl.when(jnp.logical_and(step == 0, half == 0))
-            def _():
-                pack_z(1, 0)
-                send_z(1, 0)
-
-            return c
-
         insert_y(step)
         insert_z(step, 0)
+        insert_z(step, 1)
+        lax.fori_loop(0, PX // 2 - 1, pair, 0)
 
         @pl.when(step == 0)
         def _():
-            insert_z(0, 1)
+            tiles = (blank,) * 2
+            for x in range(1, PX - 1):
+                tiles = pack_columns(1, x, tiles)
             insert_x(0)
             for x in (0, PX - 1):
                 step_plane(0, x)
             pack_xz(1)
             send(1, EDGES_XZ)
-            step_plane(0, PX // 2 - 1)
-            tiles = (blank,) * 2
             for x in (0, PX - 1):
                 tiles = pack_columns(1, x, tiles)
             pack_x(1, tiles)
             send(1, EDGES_XY + FACES_X)
-
-        lax.fori_loop(0, 2, part, 0)
-
-        @pl.when(step == 0)
-        def _():
+            pack_z(1, 0)
             pack_z(1, 1)
+            send_z(1, 0)
             send_z(1, 1)
-            tiles = (xy_out[1, 0], xy_out[1, 1])
-            for x in range(1, PX - 1):
-                tiles = pack_columns(1, x, tiles)
             pack_near(1, tiles)
             send(1, NEAR)
             for group in range(5):
@@ -423,12 +405,29 @@
         copy.wait()
     relay()
     lax.fori_loop(0, 2, one_step, 0)
-    insert_x(1)
     for group in range(4):
         whole(1, group).wait_send()
-
-
-def last_kernel(field, sens, rho, vel, por, node, out_hbm, out_sens_hbm, result, gained, sem):
+    whole(1, GROUP_FAR).wait_recv()
+
+
+def outer_plane(far, i):
+    cx, cy, cz = VELOCITIES[i]
+    s = side(-cx)
+    value = far[1, len(CORNERS) + 5 * s + CROSS_X[s].index(i)]
+    if cz:
+        line = far[1, CORNERS.index((-cx, 0, -cz)), pl.ds(s * (PZ - 1), 1), :]
+        row = lax.broadcasted_iota(jnp.int32, (PZ, PY), 0)
+        value = jnp.where(row == side(-cz) * (PZ - 1), line, value)
+    if cy:
+        edge = PY - 1 if cy == 1 else 0
+        at = CROSS_Y[side(-cy)].index(i) * PX + s * (PX - 1)
+        lane = lax.broadcasted_iota(jnp.int32, (PZ, PY), 1)
+        column = pltpu.roll(far[1, CORNERS.index((-cx, -cy, 0))], (edge - at) % PY, axis=1)
+        value = jnp.where(lane == edge, column, pltpu.roll(value, PY - 1 if cy == 1 else 1, axis=1))
+    return value
+
+
+def last_kernel(field, sens, rho, vel, por, node, far, out_hbm, out_sens_hbm, result, gained, sem):
     inner = pl.ds(PZ, ROWS - 2 * PZ)
     copies = [
         pltpu.make_async_copy(
@@ -439,7 +438,12 @@
     for copy in copies:
         copy.start()
     for k, x in enumerate((0, PX - 1)):
-        old = [field[1, i, plane(x + 1 + c[0]), :] for i, c in enumerate(VELOCITIES)]
+        old = []
+        for i, (cx, _, _) in enumerate(VELOCITIES):
+            if 0 <= x + cx < PX:
+                old.append(field[1, i, plane(x + 1 + cx), :])
+            else:
+                old.append(outer_plane(far, i))
         rows = plane(x)
         new, gain = advance(old, rows, rho, vel, por, node)
         for i in range(19):
@@ -473,16 +477,16 @@
             pltpu.VMEM((3, ROWS, PY), f32),
             pltpu.VMEM((ROWS, PY), f32),
             pltpu.VMEM((ROWS, PY), jnp.int32),
+            pltpu.VMEM((2, len(CORNERS) + 10, PZ, PY), f32),
         ),
         in_specs=[anywhere] * 6,
-        out_specs=(vmem,) * 6,
+        out_specs=(vmem,) * 7,
         scratch_shapes=[
             pltpu.VMEM((2, 2, 5, PZ, PY), f32),
             pltpu.VMEM((2, 2, PZ, PY), f32),
             pltpu.VMEM((2, 2, 2, 5, PX // 2, PY), f32),
             pltpu.VMEM((2, 2, PZ, PY), f32),
             pltpu.VMEM((2, 2, PZ, PY), f32),
-            pltpu.VMEM((2, len(CORNERS) + 10, PZ, PY), f32),
             pltpu.VMEM((2, len(NEAR), PZ, PY), f32),
             pltpu.VMEM((2, 2, 2, 5, PX // 2, PY), f32),
             pltpu.VMEM((2, PZ, PY), f32),
@@ -507,7 +511,7 @@
             jax.ShapeDtypeStruct((19, ROWS, PY), f32),
             jax.ShapeDtypeStruct((ROWS, PY), f32),
         ),
-        in_specs=[vmem] * 6,
+        in_specs=[vmem] * 7,
         out_specs=(anywhere, anywhere),
         scratch_shapes=[
             pltpu.VMEM((2, 19, PZ, PY), f32),

time: 28 us -> 27.9 us (level)
  no operation moved by 1% of the time
where the time goes in v6:
time: 27.9 us; the launch traced here: 27.8 us
  Pallas kernels  27.1 us (97%)
  between operations  0.64 us (2%)
    pallas_call x1, Pallas kernels, shards(): pl.pallas_call(lattice_kernel, out_shape=(pltpu.VMEM((3, 19, ROWS + 2 * P...  26 us
    pallas_call x1, Pallas kernels, shards(): pl.pallas_call(last_kernel, out_shape=(jax.ShapeDtypeStruct((19, ROWS, PY...  1.11 us

profile of v6, /device:TPU:1, one launch (start us, length us, event | category | flops | bytes accessed | tf_op | source)
XLA Modules:
  0.0 27.8 jit_solution(1437238702011295966)
XLA Ops:
  0.6 26.0 %shard_map.77 = (f32[3,19,144,128]{3,2,1,0:T(8,128)S(1)}, f32[3,128,128]{2,1,0:T(8,128)S(1)}, f32[128,128]{1,0:T(8,128)S(1)}, f32[3,128,128]{2,1,0:T(8,128)S(1)}...) custom-call(f32[19,128,128]{2,1,0:T(8,128)} %bitcast.8, f32[128,128]{1,0:T(8,128)} %bitcast.10, ...), custom_call_target="tpu_custom_call" | custom-call | tf_op jit(solution)/shard_map/pallas_call | solution.py:471
  26.7 1.1 %shard_map.78 = (f32[19,128,128]{2,1,0:T(8,128)}, f32[128,128]{1,0:T(8,128)}) custom-call(f32[3,19,144,128]{3,2,1,0:T(8,128)S(1)} %get-tuple-element.11.field, f32[3,128,128]{2,1,0:T(8,128)S(1)} %get-tuple-element.12.sens, f32[128,128]{1,0:T(8,128)S(1)} %get-tuple-element.13.rho, f32[3,128,128]{2,1,0:T(8,128)S(1)} %get-tuple-element.14.vel, ...), custom_call_target="tpu_custom_call" | custom-call | tf_op jit(solution)/shard_map/pallas_call | solution.py:508

commit v7 on v6

--- a/solution.py
+++ b/solution.py
@@ -44,7 +44,7 @@
 NEAR = EDGES_YZ + FACES_Y
 ROUTES = FAR + FACES_Z + NEAR
 CORNERS = EDGES_XZ + EDGES_XY
-GROUP_FAR, GROUP_Z, GROUP_NEAR, GROUP_RELAY = 0, 1, 3, 4
+GROUP_FAR, GROUP_Z, GROUP_NEAR, GROUP_RELAY = 0, 1, 2, 3
 GREETED = FACES_X + FACES_Z + NEAR
 
 
@@ -205,12 +205,12 @@
             device_id_type=pl.DeviceIdType.MESH,
         )
 
-    def transfer(step, route, half=0):
+    def transfer(step, route):
         dx, dy, dz = route
         if route in FACES_X:
             src, dst = x_out.at[step, side(dx)], x_part(far_in, step, side(dx))
         elif route in FACES_Z:
-            src, dst = z_out.at[step, half, side(dz)], z_in.at[step, half, side(dz)]
+            src, dst = z_out.at[step, side(dz)], z_in.at[step, side(dz)]
         elif route in NEAR:
             src, dst = y_out.at[step, side(dy)], near_in.at[step, NEAR.index(route)]
         elif route in EDGES_XY:
@@ -218,7 +218,7 @@
         else:
             src, dst = xz_out.at[step, side(dz)], far_in.at[step, CORNERS.index(route)]
         if route in FACES_Z:
-            return copy_of(step, GROUP_Z + half, src, dst, route)
+            return copy_of(step, GROUP_Z, src, dst, route)
         return copy_of(step, GROUP_NEAR if route in NEAR else GROUP_FAR, src, dst, route)
 
     def whole(step, group):
@@ -229,7 +229,7 @@
         elif group == GROUP_RELAY:
             buffer = relay_in
         else:
-            buffer = z_in.at[step, group - GROUP_Z]
+            buffer = z_in.at[step]
         return copy_of(step, group, buffer, buffer, FACES_X[0])
 
     def pack_xz(step):
@@ -264,17 +264,17 @@
             for j, i in enumerate(CROSS_X[s]):
                 x_out[step, s, j] = field[step, i, plane(PX if s else 1), :]
 
-    def z_rows(s, half):
-        return pl.ds(PZ + s * (PZ - 1) + half * (ROWS // 2), PX // 2, stride=PZ)
-
-    def pack_z(step, half):
+    def z_rows(s):
+        return pl.ds(PZ + s * (PZ - 1), PX, stride=PZ)
+
+    def pack_z(step):
         for s in range(2):
             for j, i in enumerate(CROSS_Z[s]):
-                z_out[step, half, s, j] = field[step, i, z_rows(s, half), :]
-
-    def send_z(step, half):
+                z_out[step, s, j] = field[step, i, z_rows(s), :]
+
+    def send_z(step):
         for route in FACES_Z:
-            transfer(step, route, half).start()
+            transfer(step, route).start()
 
     def pack_near(step, tiles):
         for s in range(2):
@@ -306,17 +306,18 @@
 
         lax.fori_loop(0, PX, body, 0, unroll=4)
 
-    def insert_z(step, half):
-        whole(step, GROUP_Z + half).wait_recv()
+    def insert_z(step):
+        wide = lax.broadcasted_iota(jnp.int32, (PX, PY), 1)
+        whole(step, GROUP_Z).wait_recv()
         for s in range(2):
             for j, i in enumerate(CROSS_Z[s]):
-                rows = z_rows(s, half)
-                value = z_in[step, half, s, j]
+                rows = z_rows(s)
+                value = z_in[step, s, j]
                 cy = VELOCITIES[i][1]
                 if cy:
                     value = pltpu.roll(value, PY - 1 if cy == 1 else 1, axis=1)
                     value = jnp.where(
-                        lane == (PY - 1 if cy == 1 else 0), field[step, i, rows, :], value
+                        wide == (PY - 1 if cy == 1 else 0), field[step, i, rows, :], value
                     )
                 field[step, i, rows, :] = value
 
@@ -356,8 +357,7 @@
             return c
 
         insert_y(step)
-        insert_z(step, 0)
-        insert_z(step, 1)
+        insert_z(step)
         lax.fori_loop(0, PX // 2 - 1, pair, 0)
 
         @pl.when(step == 0)
@@ -374,13 +374,11 @@
                 tiles = pack_columns(1, x, tiles)
             pack_x(1, tiles)
             send(1, EDGES_XY + FACES_X)
-            pack_z(1, 0)
-            pack_z(1, 1)
-            send_z(1, 0)
-            send_z(1, 1)
+            pack_z(1)
+            send_z(1)
             pack_near(1, tiles)
             send(1, NEAR)
-            for group in range(5):
+            for group in range(4):
                 whole(0, group).wait_send()
 
         return carry
@@ -393,19 +391,17 @@
     pack_xz(0)
     pack_x(0, tiles)
     pack_near(0, tiles)
-    pack_z(0, 0)
-    pack_z(0, 1)
+    pack_z(0)
     pl.semaphore_wait(barrier, len(GREETED))
     send_corner_rows()
     send(0, NEAR)
-    send_z(0, 0)
-    send_z(0, 1)
+    send_z(0)
     send(0, FACES_X)
     for copy in loads[1:]:
         copy.wait()
     relay()
     lax.fori_loop(0, 2, one_step, 0)
-    for group in range(4):
+    for group in range(3):
         whole(1, group).wait_send()
     whole(1, GROUP_FAR).wait_recv()
 
@@ -484,15 +480,15 @@
         scratch_shapes=[
             pltpu.VMEM((2, 2, 5, PZ, PY), f32),
             pltpu.VMEM((2, 2, PZ, PY), f32),
-            pltpu.VMEM((2, 2, 2, 5, PX // 2, PY), f32),
+            pltpu.VMEM((2, 2, 5, PX, PY), f32),
             pltpu.VMEM((2, 2, PZ, PY), f32),
             pltpu.VMEM((2, 2, PZ, PY), f32),
             pltpu.VMEM((2, len(NEAR), PZ, PY), f32),
-            pltpu.VMEM((2, 2, 2, 5, PX // 2, PY), f32),
+            pltpu.VMEM((2, 2, 5, PX, PY), f32),
             pltpu.VMEM((2, PZ, PY), f32),
             dma((6,)),
-            dma((2, 5)),
-            dma((2, 5)),
+            dma((2, 4)),
+            dma((2, 4)),
         ],
         compiler_params=pltpu.CompilerParams(
             collective_id=0, has_side_effects=True, vmem_limit_bytes=56 * 1024 * 1024

time: 27.9 us -> 27.8 us (level)
  no operation moved by 1% of the time
where the time goes in v7:
time: 27.8 us; the launch traced here: 27.7 us
  Pallas kernels  27 us (97%)
  between operations  0.64 us (2%)
    pallas_call x1, Pallas kernels, shards(): pl.pallas_call(lattice_kernel, out_shape=(pltpu.VMEM((3, 19, ROWS + 2 * P...  25.9 us
    pallas_call x1, Pallas kernels, shards(): pl.pallas_call(last_kernel, out_shape=(jax.ShapeDtypeStruct((19, ROWS, PY...  1.11 us

profile of v7, /device:TPU:1, one launch (start us, length us, event | category | flops | bytes accessed | tf_op | source)
XLA Modules:
  0.0 27.7 jit_solution(5561261038719388872)
XLA Ops:
  0.6 25.9 %shard_map.77 = (f32[3,19,144,128]{3,2,1,0:T(8,128)S(1)}, f32[3,128,128]{2,1,0:T(8,128)S(1)}, f32[128,128]{1,0:T(8,128)S(1)}, f32[3,128,128]{2,1,0:T(8,128)S(1)}...) custom-call(f32[19,128,128]{2,1,0:T(8,128)} %bitcast.8, f32[128,128]{1,0:T(8,128)} %bitcast.10, ...), custom_call_target="tpu_custom_call" | custom-call | tf_op jit(solution)/shard_map/pallas_call | solution.py:467
  26.6 1.1 %shard_map.78 = (f32[19,128,128]{2,1,0:T(8,128)}, f32[128,128]{1,0:T(8,128)}) custom-call(f32[3,19,144,128]{3,2,1,0:T(8,128)S(1)} %get-tuple-element.11.field, f32[3,128,128]{2,1,0:T(8,128)S(1)} %get-tuple-element.12.sens, f32[128,128]{1,0:T(8,128)S(1)} %get-tuple-element.13.rho, f32[3,128,128]{2,1,0:T(8,128)S(1)} %get-tuple-element.14.vel, ...), custom_call_target="tpu_custom_call" | custom-call | tf_op jit(solution)/shard_map/pallas_call | solution.py:504
